TPU v7x, 512 devices: a whole 4x4x16 slice. The times are simulated.
512 devices in a mesh: row: 16 (over y, x), col: 32 (over z, core).
Axes of the slice: x: 4, y: 4, z: 16, core: 2. Of those that a mesh axis runs over, the one named last changes fastest.
Arguments:
- matrix: float32 [16, 8, 128, 32, 4, 128], P('row', None, None, 'col'), as said below
Outputs:
- factored: float32 [16, 8, 128, 32, 4, 128], P('row', None, None, 'col')
Inputs may be any that keep to these rules, and one draw needn't show every extreme that they name: matrix is a Gaussian-process covariance matrix with a nugget term: symmetric and positive definite.
All inputs are finite; a program needn't handle non-finite values.
Results may differ from a plain program's by a relative error of at most 0.0003.
Values sent between devices are 32-bit elements; how exact they have to be, the bound alone decides.
No kernel may reach another device: no remote copies, remote signals or barrier semaphores. Data moves between devices by JAX's collectives and lax.ppermute only.
A program may use at most 64 MiB of HBM per device.

v0:
```python
import jax
import jax.numpy as jnp
from jax import lax
from jax.sharding import PartitionSpec as P

STEPS = 2


def from_root(value, axis, source):
    kept = jnp.where(lax.axis_index(axis) == source, value, 0).astype(value.dtype)
    return lax.psum(kept, axis)


def rank_update(store, panel, mirrored, keep):
    update = jnp.einsum("xai,ybi->xayb", panel, mirrored, precision=lax.Precision.HIGHEST)
    return store - jnp.where(keep, update, 0.0)


def shards(matrix):
    row_count = lax.axis_size("row")
    col_count = lax.axis_size("col")
    my_row = lax.axis_index("row")
    my_col = lax.axis_index("col")
    row_blocks = matrix.shape[1]
    width = matrix.shape[2]
    col_blocks = matrix.shape[4]
    store = matrix.reshape(row_blocks, width, col_blocks, width)
    grow = jnp.arange(row_blocks, dtype=jnp.int32) * row_count + my_row
    gcol = jnp.arange(col_blocks, dtype=jnp.int32) * col_count + my_col
    lower = grow[:, None, None, None] >= gcol[None, None, :, None]
    identity = jnp.eye(width, dtype=jnp.float32)
    pending = None
    for step in range(STEPS):
        local_col = step // col_count
        column = from_root(store[:, :, local_col, :], "col", step % col_count)
        diagonal = from_root(column[step // row_count], "row", step % row_count)
        factor = jnp.linalg.cholesky(diagonal)
        inverse = lax.linalg.triangular_solve(factor, identity, left_side=True, lower=True)
        solved = jnp.einsum("xai,bi->xab", column, inverse, precision=lax.Precision.HIGHEST)
        below = (grow > step)[:, None, None]
        panel = jnp.where(below, solved, 0.0)
        written = jnp.where(
            below, solved, jnp.where((grow == step)[:, None, None], factor[None], column)
        )
        owner = my_col == step % col_count
        store = store.at[:, :, local_col, :].set(
            jnp.where(owner, written, store[:, :, local_col, :])
        )
        selected = (
            jnp.arange(col_blocks, dtype=jnp.int32) * (col_count // row_count) + my_col // row_count
        )
        mirrored = from_root(jnp.take(panel, selected, axis=0), "row", my_col % row_count)
        store = rank_update(store, panel, mirrored, lower)
        pending = None
    row_ids = grow[:, None] * width + jnp.arange(width, dtype=jnp.int32)[None, :]
    col_ids = gcol[:, None] * width + jnp.arange(width, dtype=jnp.int32)[None, :]
    triangle = row_ids[:, :, None, None] >= col_ids[None, None, :, :]
    result = jnp.where(triangle, store, 0.0)
    return result.reshape(1, row_blocks, width, 1, col_blocks, width)


def solution(mesh):
    in_specs = (P("row", None, None, "col", None, None),)
    out_specs = P("row", None, None, "col", None, None)
    return jax.shard_map(shards, mesh=mesh, in_specs=in_specs, out_specs=out_specs, check_vma=False)
```

profile of v0, /device:TPU:1, one launch (start us, length us, event | category | flops | bytes accessed | tf_op | source)
XLA Modules:
  0.0 963.0 jit_solution(6912074096477813561)
XLA Ops:
  6.5 0.0 all-reduce.7.cloned.1.call-start
  6.5 1.9 copy.2
  8.5 0.8 fusion.2
  9.3 0.0 all-reduce.7.cloned.1.call-update
  9.3 0.0 all-reduce.9.cloned.1.call-start
  9.5 213.4 %all-reduce.7.cloned.1.call-done = f32[8,128,128]{1,2,0:T(8,128)} async-done(((f32[8,128,128]{1,2,0:T(8,128)}), f32[8,128,128]{1,2,0:T(8,128)}) %all-reduce.7.cloned.1.call-update) | async-done | bytes 524304 | tf_op jit(solution)/shard_map/psum | solution.py:11
  223.0 1.5 fusion.9
  224.5 0.0 all-reduce.9.cloned.1.call-update
  224.5 0.0 all-reduce.11.cloned.1.call-start
  224.5 111.8 %all-reduce.9.cloned.1.call-done = f32[128,128]{0,1:T(8,128)} async-done(((f32[128,128]{0,1:T(8,128)}), f32[128,128]{0,1:T(8,128)}) %all-reduce.9.cloned.1.call-update) | async-done | bytes 65552 | tf_op jit(solution)/shard_map/psum | solution.py:11
  336.3 0.9 copy.3
  337.3 0.9 fusion.13
  338.1 11.7 %cholesky.44 = f32[128,128]{1,0:T(8,128)S(1)} custom-call(f32[128,128]{1,0:T(8,128)S(1)} %fusion.13), custom_call_target="Cholesky" | custom-call | tf_op jit(solution)/shard_map/jit(cholesky)/cholesky | solution.py:37
  349.9 0.6 compare_reduce_fusion.1
  350.5 0.7 select_bitcast_fusion.2
  351.2 9.8 %custom-call.6 = f32[1,128,128]{1,2,0:T(8,128)S(1)} custom-call(f32[1,128,128]{2,1,0:T(8,128)S(1)} %get-tuple-element.34), custom_call_target="InvertDiagBlocksLowerTriangular" | custom-call | tf_op jit(solution)/shard_map/triangular_solve/custom-call.0 | solution.py:38
  361.0 0.3 convolution_bitcast_fusion.1
  361.3 0.1 copy.5
  361.4 1.8 bitcast_dynamic-update-slice_fusion.1
  363.2 0.1 broadcast_select_fusion.1
  363.3 0.6 gather_fusion
  363.9 0.8 select_select_fusion.1
  364.7 0.0 all-reduce.11.cloned.1.call-update
  364.7 0.0 all-reduce.13.cloned.1.call-start
  364.8 0.1 broadcast_compare_fusion
  364.9 114.8 %all-reduce.11.cloned.1.call-done = f32[4,128,128]{1,2,0:T(8,128)} async-done(((f32[4,128,128]{1,2,0:T(8,128)}), f32[4,128,128]{1,2,0:T(8,128)}) %all-reduce.11.cloned.1.call-update) | async-done | bytes 262160 | tf_op jit(solution)/shard_map/psum | solution.py:11
  479.7 2.9 select_subtract_fusion
  482.5 0.0 copy-start
  482.5 1.3 copy-done
  483.8 0.8 fusion.3
  484.7 0.0 copy-start.1
  484.7 0.0 all-reduce.13.cloned.1.call-update
  484.7 0.0 all-reduce.15.cloned.1.call-start
  484.8 0.1 iota_add_fusion.1
  484.9 208.9 %all-reduce.13.cloned.1.call-done = f32[8,128,128]{1,2,0:T(8,128)} async-done(((f32[8,128,128]{1,2,0:T(8,128)}), f32[8,128,128]{1,2,0:T(8,128)}) %all-reduce.13.cloned.1.call-update) | async-done | bytes 524304 | tf_op jit(solution)/shard_map/psum | solution.py:11
  693.7 0.0 copy-start.2
  693.8 1.5 fusion.8
  695.3 0.0 all-reduce.15.cloned.1.call-update
  695.3 0.2 all-reduce.17.cloned.1.call-start
  695.5 1.1 slice_bitcast_fusion
  696.6 110.0 %all-reduce.15.cloned.1.call-done = f32[128,128]{0,1:T(8,128)} async-done(((f32[128,128]{0,1:T(8,128)}), f32[128,128]{0,1:T(8,128)}) %all-reduce.15.cloned.1.call-update) | async-done | bytes 65552 | tf_op jit(solution)/shard_map/psum | solution.py:11
  806.6 0.9 copy.11
  807.5 0.9 fusion.11
  808.4 11.7 %cholesky.55 = f32[128,128]{1,0:T(8,128)S(1)} custom-call(f32[128,128]{1,0:T(8,128)S(1)} %fusion.11), custom_call_target="Cholesky" | custom-call | tf_op jit(solution)/shard_map/jit(cholesky)/cholesky | solution.py:37
  820.1 0.7 compare_reduce_fusion
  820.9 0.7 select_bitcast_fusion.1
  821.6 9.8 %custom-call.7 = f32[1,128,128]{1,2,0:T(8,128)S(1)} custom-call(f32[1,128,128]{2,1,0:T(8,128)S(1)} %get-tuple-element.32), custom_call_target="InvertDiagBlocksLowerTriangular" | custom-call | tf_op jit(solution)/shard_map/triangular_solve/custom-call.0 | solution.py:38
  831.4 0.3 convolution_bitcast_fusion
  831.7 0.1 copy.13
  831.8 0.0 copy-done.1
  831.8 0.0 copy-done.2
  831.8 0.6 bitcast_dynamic-update-slice_fusion
  832.4 0.1 broadcast_select_fusion
  832.6 0.6 gather_fusion.1
  833.1 0.8 select_select_fusion
  833.9 0.0 all-reduce.17.cloned.1.call-update
  834.0 0.1 iota_add_fusion
  834.0 114.9 %all-reduce.17.cloned.1.call-done = f32[4,128,128]{1,2,0:T(8,128)} async-done(((f32[4,128,128]{1,2,0:T(8,128)}), f32[4,128,128]{1,2,0:T(8,128)}) %all-reduce.17.cloned.1.call-update) | async-done | bytes 262160 | tf_op jit(solution)/shard_map/psum | solution.py:11
  948.9 4.3 select_bitcast_fusion
  953.2 2.9 copy.19
  (12 shorter events, 0.2 us)
Async XLA Ops:
  6.5 216.4 %all-reduce.7.cloned.1.call-start = ((), (), s32[]{:S(2)}) async-start(), calls=%async_computation | async-start | bytes 1048576 | tf_op jit(solution)/shard_map/psum | solution.py:11
  9.3 327.0 %all-reduce.9.cloned.1.call-start = ((), (), s32[]{:S(2)}) async-start(), calls=%async_computation.1 | async-start | bytes 131072 | tf_op jit(solution)/shard_map/psum | solution.py:11
  224.5 255.2 %all-reduce.11.cloned.1.call-start = ((), (), s32[]{:S(2)}) async-start(), calls=%async_computation.2 | async-start | bytes 524288 | tf_op jit(solution)/shard_map/psum | solution.py:11
  364.7 329.0 %all-reduce.13.cloned.1.call-start = ((), (), s32[]{:S(2)}) async-start(), calls=%async_computation.3 | async-start | bytes 1048576 | tf_op jit(solution)/shard_map/psum | solution.py:11
  482.5 1.3 copy-start
  484.7 347.1 %copy-start.1 = (f32[8,128,4,128]{1,3,0,2:T(8,128)S(1)}, f32[8,128,4,128]{1,3,0,2:T(8,128)}, u32[]{:S(2)}) copy-start(f32[8,128,4,128]{1,3,0,2:T(8,128)} %copy-done) | copy-start | bytes 6291460
  484.7 321.9 %all-reduce.15.cloned.1.call-start = ((), (), s32[]{:S(2)}) async-start(), calls=%async_computation.4 | async-start | bytes 131072 | tf_op jit(solution)/shard_map/psum | solution.py:11
  693.7 138.0 %copy-start.2 = (f32[8,128,128]{1,2,0:T(8,128)S(1)}, f32[8,128,128]{1,2,0:T(8,128)}, u32[]{:S(2)}) copy-start(f32[8,128,128]{1,2,0:T(8,128)} %all-reduce.13.cloned.1.call-done) | copy-start | bytes 1572868
  695.3 253.6 %all-reduce.17.cloned.1.call-start = ((), (), s32[]{:S(2)}) async-start(), calls=%async_computation.5 | async-start | bytes 524288 | tf_op jit(solution)/shard_map/psum | solution.py:11
Sparse Core Ops, SparseCore 0:
  9.7 213.2 all-reduce.6
  226.5 109.7 all-reduce.8
  364.9 114.7 all-reduce.10
  484.8 208.8 all-reduce.12
  696.8 109.7 all-reduce.14
  834.1 114.7 all-reduce.16
where the time goes:
time: 964 us; the launch traced here: 963 us
  waiting for transfers between devices  874 us (91%)
  other arithmetic  54.3 us (6%)
  between operations  13.8 us (1%)
  local copies, waits for them, and re-layouts  10.4 us (1%)
  matrix products  10.3 us (1%)
    psum x6, waiting for transfers between devices, from_root(): return lax.psum(kept, axis)  874 us
    another operation x6, other arithmetic, shards(): factor = jnp.linalg.cholesky(diagonal)  24.9 us
    another operation x4, other arithmetic, shards(): lax.linalg.triangular_solve(factor, identity, left_side=True, lower=True)  21 us
  transfers between devices with their start and end apart: 6, of which 6 were waited for; matrix products, arithmetic and copies ran while one was open for 0% of the time, Pallas kernels for 0%

commit v1 on v0

v1 whole, which is shorter than its diff:
```python
import jax
import jax.numpy as jnp
from jax import lax
from jax.experimental import pallas as pl
from jax.experimental.pallas import tpu as pltpu
from jax.sharding import PartitionSpec as P

HIGHEST = lax.Precision.HIGHEST
ROWS = 16
COLS = 32
LAYERS = 16
NB = 128
HALF = 64
PIECE = 8
STEP_ROWS = 256


def mm(a, b):
    return lax.dot_general(
        a, b, (((1,), (0,)), ((), ())), precision=HIGHEST, preferred_element_type=jnp.float32
    )


def mmt(a, b):
    return lax.dot_general(
        a, b, (((1,), (1,)), ((), ())), precision=HIGHEST, preferred_element_type=jnp.float32
    )


def eliminate(block, work):
    n = HALF
    shape = (8, 2 * n)
    lane = lax.broadcasted_iota(jnp.int32, shape, 1)
    sub = lax.broadcasted_iota(jnp.int32, shape, 0)
    work[:, :n] = block
    parts = []
    for i in range(n // 8):
        unit = jnp.where(lane == n + 8 * i + sub, 1.0, 0.0)
        parts.append(jnp.where(lane < n, work[8 * i : 8 * i + 8, :], unit))
    out = []
    for a in range(n // 8):
        rest = range(a + 1, n // 8)
        cols = []
        for j in range(8):
            k = 8 * a + j
            cols.append(
                {i: jnp.broadcast_to(parts[i][:, k : k + 1], shape) for i in range(a, n // 8)}
            )
        e = [
            [jnp.broadcast_to(cols[j][a][i : i + 1, :], shape) for j in range(i + 1)]
            for i in range(8)
        ]
        rows = [jnp.broadcast_to(parts[a][k : k + 1, :], shape) for k in range(8)]
        strip = None
        for k in range(8):
            inv = 1.0 / e[k][k]
            for i in range(k + 1, 8):
                low = e[i][k] * inv
                for j in range(k + 1, i + 1):
                    e[i][j] = e[i][j] - low * e[j][k]
                rows[i] = rows[i] - low * rows[k]
            root = lax.rsqrt(e[k][k])
            root = root * (1.5 - 0.5 * e[k][k] * root * root)
            done = rows[k] * root
            strip = done if k == 0 else jnp.where(sub == k, done, strip)
            for i in rest:
                m = cols[k][i] * inv
                for j in range(k + 1, 8):
                    cols[j][i] = cols[j][i] - m * e[j][k]
                parts[i] = parts[i] - m * rows[k]
        out.append(strip)
    full = jnp.concatenate(out, axis=0)
    r = lax.broadcasted_iota(jnp.int32, (n, n), 0)
    c = lax.broadcasted_iota(jnp.int32, (n, n), 1)
    return jnp.where(r <= c, full[:, :n], 0.0), jnp.where(r >= c, full[:, n:], 0.0)


def factor_block(s, work, upper):
    h = HALF
    u11, i11 = eliminate(s[:h, :h], work)
    l21 = mmt(s[h:, :h], i11)
    t21 = mm(l21, i11)
    u22, i22 = eliminate(s[h:, h:] - mmt(l21, l21), work)
    upper[:h, :h] = u11
    upper[:h, h:] = l21.T
    upper[h:, :h] = jnp.zeros((h, h), jnp.float32)
    upper[h:, h:] = u22
    return i11, -mm(i22, t21), i22


def factor_kernel(place, own, other, inv, l11, l21, l22, work, upper):
    h, n = HALF, NB
    even = place[1] % 2 == 0

    def block(side, half):
        a, b = own[:, half].reshape(n, n), other[:, half].reshape(n, n)
        return jnp.where(even, a, b) if side == 0 else jnp.where(even, b, a)

    def put(o, blocks):
        inv[o : o + h, o : o + h] = blocks[0]
        inv[o : o + h, o + h : o + n] = jnp.zeros((h, h), jnp.float32)
        inv[o + h : o + n, o : o + h] = blocks[1]
        inv[o + h : o + n, o + h : o + n] = blocks[2]

    put(0, factor_block(block(0, 0), work, upper))
    l11[...] = upper[...].T
    i11 = inv[:n, :n]
    p = mmt(block(0, 1), i11)
    t = mm(p, i11)
    l21[...] = p
    put(n, factor_block(block(1, 1) - mmt(p, p), work, upper))
    l22[...] = upper[...].T
    inv[:n, n:] = jnp.zeros((n, n), jnp.float32)
    inv[n:, :n] = -mm(inv[n:, n:], t)


def factorise(place, own, other):
    block = jax.ShapeDtypeStruct((NB, NB), jnp.float32)
    whole = jax.ShapeDtypeStruct((2 * NB, 2 * NB), jnp.float32)
    vmem = pl.BlockSpec(memory_space=pltpu.VMEM)
    return pl.pallas_call(
        factor_kernel,
        in_specs=[pl.BlockSpec(memory_space=pltpu.SMEM), vmem, vmem],
        out_specs=[vmem] * 4,
        out_shape=[whole, block, block, block],
        scratch_shapes=[pltpu.VMEM((HALF, NB), jnp.float32), pltpu.VMEM((NB, NB), jnp.float32)],
        name="factorise",
    )(place, own, other)


def update_kernel(place, inv, l11, l21, l22, own, other, strips, store, out, mirrored):
    n = NB
    step = pl.program_id(0)
    row, col = place[0], place[1]
    even = col % 2 == 0

    @pl.when(step == 0)
    def _():
        top = [[] for _ in range(4)]
        for half in range(2):
            for j in range(4):
                for p in range(ROWS):
                    top[j].append(strips[p, half, pl.ds(j, PIECE, stride=4), :])
        whole = jnp.concatenate([jnp.concatenate(t, axis=0) for t in top], axis=1)
        mirrored[...] = mm(inv[...], whole)

    a, b = own[...], other[...]
    left, right = jnp.where(even, a, b), jnp.where(even, b, a)
    panel = mmt(jnp.concatenate([left, right], axis=1), inv[...])
    update = mm(panel, mirrored[...])
    local = lax.broadcasted_iota(jnp.int32, (STEP_ROWS, n), 0)
    grow = (step * (STEP_ROWS // n) + local // n) * ROWS + row
    rid = grow * n + local % n
    lane = lax.broadcasted_iota(jnp.int32, (STEP_ROWS, n), 1)
    for j in range(4):
        cid = (j * COLS + col) * n + lane
        rows = pl.ds(j, STEP_ROWS, stride=4)
        out[rows, :] = jnp.where(rid >= cid, store[rows, :] - update[:, j * n : (j + 1) * n], 0.0)

    @pl.when(col < 2)
    def _():
        first = jnp.where(col == 0, l11[...], 0.0)
        second = jnp.where(col == 0, l21[...], l22[...])
        pad = jnp.zeros((STEP_ROWS - n, n), jnp.float32)
        solved = jnp.where(col == 0, panel[:, :n], panel[:, n:])
        solved = jnp.where(grow == 0, jnp.concatenate([first, pad], axis=0), solved)
        solved = jnp.where(grow == 1, jnp.concatenate([second, pad], axis=0), solved)
        out[pl.ds(0, STEP_ROWS, stride=4), :] = jnp.where(rid >= col * n + lane, solved, 0.0)


def update(place, inv, l11, l21, l22, own, other, strips, view):
    fixed = pl.BlockSpec(memory_space=pltpu.VMEM)
    rows = pl.BlockSpec((STEP_ROWS, NB), lambda i: (i, 0))
    wide = pl.BlockSpec((4 * STEP_ROWS, NB), lambda i: (i, 0))
    return pl.pallas_call(
        update_kernel,
        grid=(view.shape[0] // (4 * STEP_ROWS),),
        in_specs=[pl.BlockSpec(memory_space=pltpu.SMEM)] + [fixed] * 4 + [rows, rows, fixed, wide],
        out_specs=wide,
        out_shape=jax.ShapeDtypeStruct(view.shape, jnp.float32),
        scratch_shapes=[pltpu.VMEM((2 * NB, 4 * NB), jnp.float32)],
        name="update",
    )(place, inv, l11, l21, l22, own, other, strips, view)


def z_pairs(held, stride):
    pairs = []
    for z in held:
        pairs.append((2 * z, 2 * ((z + stride) % LAYERS)))
        pairs.append((2 * z + 1, 2 * ((z - stride) % LAYERS) + 1))
    return pairs


def swap_core(value):
    return lax.ppermute(value, "col", [(c, c ^ 1) for c in range(COLS)])


def shards(matrix):
    row = lax.axis_index("row")
    col = lax.axis_index("col")
    place = jnp.stack([row, col])
    layer = jnp.where(col % 2 == 0, col // 2, (LAYERS - col // 2) % LAYERS)
    view = matrix.reshape(-1, NB)
    column = view.reshape(-1, 4, NB)[:, 0, :]

    def spread(value, stride, after=None):
        held = list(range(0, LAYERS, 2 * stride))
        moved = lax.ppermute(value, "col", z_pairs(held, stride))
        if after is not None:
            value, moved, _ = lax.optimization_barrier((value, moved, after))
        return jnp.where(layer % (2 * stride) == stride, moved, value)

    pieces = view[: 4 * NB].reshape(ROWS, 4 * PIECE, NB)
    pieces = lax.all_to_all(pieces, "row", 0, 0, tiled=True)
    column = spread(column, 8, pieces)
    pieces = jnp.broadcast_to(pieces[:2][None], (ROWS, 2, 4 * PIECE, NB))
    pieces, column = lax.optimization_barrier((pieces, column))
    strips = lax.all_to_all(pieces, "row", 0, 0, tiled=True)
    column = spread(column, 4, strips)

    corner = strips[:, :, ::4, :]
    corner, column = lax.optimization_barrier((corner, column))
    for held, stride in (([0], 4), ([0, 4, 8, 12], 1)):
        parts = {q: lax.ppermute(corner, "col", z_pairs(held, q * stride)) for q in (2, 1, 3)}
        part = (layer // stride) % 4
        kept = jnp.where(part == 2, parts[2], corner)
        corner = jnp.where(part == 1, parts[1], jnp.where(part == 3, parts[3], kept))
        if stride == 4:
            column = spread(column, 2, corner)
            corner, column = lax.optimization_barrier((corner, column))
    corner_other = swap_core(corner)
    column = spread(column, 1, corner_other)
    corner, corner_other, column = lax.optimization_barrier((corner, corner_other, column))
    column_other = swap_core(column)
    inv, l11, l21, l22 = factorise(place, corner, corner_other)
    out = update(place, inv, l11, l21, l22, column, column_other, strips, view)
    return out.reshape(matrix.shape)


def solution(mesh):
    spec = P("row", None, None, "col", None, None)
    return jax.shard_map(shards, mesh=mesh, in_specs=(spec,), out_specs=spec, check_vma=False)
```

time: 964 us -> 110 us (0.11)
  waiting for transfers between devices: 874 us -> 26.2 us
  starting transfers between devices: 0.39 us -> 56.2 us
  other arithmetic: 54.3 us -> 0.95 us
  Pallas kernels: 0 us -> 20.3 us
  between operations: 13.8 us -> 0.4 us
  matrix products: 10.3 us -> 0 us
    psum x6 -> x0, waiting for transfers between devices: 874 us -> none  [from_root(): return lax.psum(kept, axis)]
    ppermute x0 -> x12, starting transfers between devices: none -> 45.9 us  [the longest x4 20.3 us: spread(): moved = lax.ppermute(value, 'col', z_pairs(held, stride))]
    another operation x10 -> x1, other arithmetic: 45.8 us -> 0.66 us  [shards(): place = jnp.stack([row, col])]
    pallas_call x0 -> x2, Pallas kernels: none -> 20.3 us  [the longest x1 11.9 us: factorise(): pl.pallas_call(factor_kernel, in_specs=[pl.BlockSpec(memory_space=pltpu.S...]
    all_to_all x0 -> x2, waiting for transfers between devices: none -> 17 us  [the longest x1 9.39 us: shards(): strips = lax.all_to_all(pieces, 'row', 0, 0, tiled=True)]
    all_to_all x0 -> x2, starting transfers between devices: none -> 10.3 us  [the longest x1 6.75 us: shards(): pieces = lax.all_to_all(pieces, 'row', 0, 0, tiled=True)]
    dot_general x4 -> x0, matrix products: 9.69 us -> none  [the longest x2 7.2 us: rank_update(): jnp.einsum('xai,ybi->xayb', panel, mirrored, precision=lax.Precision.HIGH...]
  transfers between devices with their start and end apart: 6 -> 14, of which waited for: 6 -> 8; matrix products, arithmetic and copies ran while one was open for 0% -> 2% of each run, Pallas kernels for 0% -> 11%
where the time goes in v1:
time: 110 us
  starting transfers between devices  56.2 us (51%)
  waiting for transfers between devices  26.2 us (24%)
  Pallas kernels  20.3 us (18%)
  local copies, waits for them, and re-layouts  5.48 us (5%)
    ppermute x4, starting transfers between devices, spread(): moved = lax.ppermute(value, 'col', z_pairs(held, stride))  20.3 us
    ppermute x6, starting transfers between devices, shards(): lax.ppermute(corner, 'col', z_pairs(held, q * stride))  17.4 us
    pallas_call x1, Pallas kernels, factorise(): pl.pallas_call(factor_kernel, in_specs=[pl.BlockSpec(memory_space=pltpu.S...  11.9 us
    all_to_all x1, waiting for transfers between devices, shards(): strips = lax.all_to_all(pieces, 'row', 0, 0, tiled=True)  9.39 us
    pallas_call x1, Pallas kernels, update(): pl.pallas_call(update_kernel, grid=(view.shape[0] // (4 * STEP_ROWS),), i...  8.5 us
    ppermute x6, waiting for transfers between devices, shards(): lax.ppermute(corner, 'col', z_pairs(held, q * stride))  8.22 us
    ppermute x2, starting transfers between devices, swap_core(): return lax.ppermute(value, 'col', [(c, c ^ 1) for c in range(COLS)])  8.21 us
    all_to_all x1, waiting for transfers between devices, shards(): pieces = lax.all_to_all(pieces, 'row', 0, 0, tiled=True)  7.61 us
  transfers between devices with their start and end apart: 14, of which 8 were waited for; matrix products, arithmetic and copies ran while one was open for 2% of the time, Pallas kernels for 11%

profile of v1, /device:TPU:1, one launch (start us, length us, event | category | flops | bytes accessed | tf_op | source)
XLA Modules:
  0.0 109.6 jit_solution(10813114918023051363)
XLA Ops:
  0.0 1.8 %copy.2 = f32[1,8,128,1,4,128]{5,2,1,4,3,0:T(8,128)S(1)} copy(f32[1,8,128,1,4,128]{5,4,3,2,1,0:T(4,128)} %param.1) | data formatting | bytes 4194304 | tf_op args[0]
  1.9 16.3 %collective-permute-start = (f32[1024,128]{1,0:T(8,128)S(1)}, f32[1024,128]{1,0:T(8,128)S(1)}, u32[]{:S(2)}, u32[]{:S(2)}) collective-permute-start(f32[1024,128]{1,0:T(8,128)S(1)} %slice_bitcast_fusion), channel_id=1, source_target_pairs={{0,16},{1,17},{32,48},{33,49},{64,80},{65,81},{96,112},{97,113},{1... | collective-permute-start | bytes 1572872 | tf_op jit(solution)/shard_map/ppermute | solution.py:208
  18.2 1.7 %slice.13 = f32[1,1,128,1,4,128]{5,4,3,2,1,0:T(4,128)} slice(f32[1,8,128,1,4,128]{5,4,3,2,1,0:T(4,128)} %param.1), slice={[0:1], [0:1], [0:128], [0:1], [0:4], [0:128]} | slice | bytes 524288 | tf_op jit(solution)/shard_map/slice | solution.py:213
  19.9 6.8 %all-to-all-start = ((f32[16,32,128]{2,1,0:T(8,128)}), f32[16,32,128]{2,1,0:T(8,128)S(1)}, u32[]{:S(2)}, u32[]{:S(2)}) async-start(f32[16,32,128]{2,1,0:T(8,128)} %bitcast.2), calls=%async_computation | async-start | bytes 524288 | tf_op jit(solution)/shard_map/all_to_all | solution.py:214
  26.7 7.6 %all-to-all-done = f32[16,32,128]{2,1,0:T(8,128)S(1)} async-done(((f32[16,32,128]{2,1,0:T(8,128)}), f32[16,32,128]{2,1,0:T(8,128)S(1)}, u32[]{:S(2)}, u32[]{:S(2)}) %all-to-all-start) | async-done | bytes 262176 | tf_op jit(solution)/shard_map/all_to_all | solution.py:214
  34.3 0.0 collective-permute-done
  34.3 0.1 broadcast_select_fusion.3
  34.4 0.9 broadcast_in_dim.2
  35.2 1.3 %collective-permute-start.1 = (f32[1024,128]{1,0:T(8,128)S(1)}, f32[1024,128]{1,0:T(8,128)S(1)}, u32[]{:S(2)}, u32[]{:S(2)}) collective-permute-start(f32[1024,128]{1,0:T(8,128)S(1)} %broadcast_select_fusion.3), channel_id=1, source_target_pairs={{0,8},{1,25},{16,24},{17,9},{32,40},{33,57},{48,56},{49,41},{64,72... | collective-permute-start | bytes 1572872 | tf_op jit(solution)/shard_map/ppermute | solution.py:208
  36.5 3.6 %all-to-all-start.1 = ((f32[16,2,32,128]{3,2,1,0:T(8,128)}), f32[16,2,32,128]{3,2,1,0:T(8,128)S(1)}, u32[]{:S(2)}, u32[]{:S(2)}) async-start(f32[16,2,32,128]{3,2,1,0:T(8,128)} %broadcast_in_dim.2), calls=%async_computation.1 | async-start | bytes 1048576 | tf_op jit(solution)/shard_map/all_to_all | solution.py:218
  40.2 9.4 %all-to-all-done.1.strips = f32[16,2,32,128]{3,2,1,0:T(8,128)S(1)} async-done(((f32[16,2,32,128]{3,2,1,0:T(8,128)}), f32[16,2,32,128]{3,2,1,0:T(8,128)S(1)}, u32[]{:S(2)}, u32[]{:S(2)}) %all-to-all-start.1) | async-done | bytes 524320 | tf_op jit(solution)/shard_map/all_to_all | solution.py:218
  49.6 0.0 copy-start
  49.6 0.3 slice.16
  49.8 0.0 collective-permute-done.1
  49.8 0.1 broadcast_select_fusion.2
  49.9 1.3 %collective-permute-start.5 = (f32[1024,128]{1,0:T(8,128)S(1)}, f32[1024,128]{1,0:T(8,128)S(1)}, u32[]{:S(2)}, u32[]{:S(2)}) collective-permute-start(f32[1024,128]{1,0:T(8,128)S(1)} %broadcast_select_fusion.2), channel_id=1, source_target_pairs={{0,4},{1,29},{8,12},{9,5},{16,20},{17,13},{24,28},{25,21},{32,36},... | collective-permute-start | bytes 1572872 | tf_op jit(solution)/shard_map/ppermute | solution.py:208
  51.2 10.9 %collective-permute-start.4 = (f32[16,2,8,128]{3,2,1,0:T(8,128)S(1)}, f32[16,2,8,128]{3,2,1,0:T(8,128)S(1)}, u32[]{:S(2)}, u32[]{:S(2)}) collective-permute-start(f32[16,2,8,128]{3,2,1,0:T(8,128)S(1)} %slice.16), channel_id=1, source_target_pairs={{0,16},{1,17},{32,48},{33,49},{64,80},{65,81},{96,112},{97,113},{1... | collective-permute-start | bytes 393224 | tf_op jit(solution)/shard_map/ppermute | solution.py:224
  62.2 1.3 %collective-permute-start.3 = (f32[16,2,8,128]{3,2,1,0:T(8,128)S(1)}, f32[16,2,8,128]{3,2,1,0:T(8,128)S(1)}, u32[]{:S(2)}, u32[]{:S(2)}) collective-permute-start(f32[16,2,8,128]{3,2,1,0:T(8,128)S(1)} %slice.16), channel_id=1, source_target_pairs={{0,24},{1,9},{32,56},{33,41},{64,88},{65,73},{96,120},{97,105},{12... | collective-permute-start | bytes 393224 | tf_op jit(solution)/shard_map/ppermute | solution.py:224
  63.5 1.3 %collective-permute-start.2 = (f32[16,2,8,128]{3,2,1,0:T(8,128)S(1)}, f32[16,2,8,128]{3,2,1,0:T(8,128)S(1)}, u32[]{:S(2)}, u32[]{:S(2)}) collective-permute-start(f32[16,2,8,128]{3,2,1,0:T(8,128)S(1)} %slice.16), channel_id=1, source_target_pairs={{0,8},{1,25},{32,40},{33,57},{64,72},{65,89},{96,104},{97,121},{12... | collective-permute-start | bytes 393224 | tf_op jit(solution)/shard_map/ppermute | solution.py:224
  64.9 0.0 collective-permute-done.4
  64.9 0.6 collective-permute-done.3
  65.5 1.2 %collective-permute-done.2 = f32[16,2,8,128]{3,2,1,0:T(8,128)S(1)} collective-permute-done((f32[16,2,8,128]{3,2,1,0:T(8,128)S(1)}, f32[16,2,8,128]{3,2,1,0:T(8,128)S(1)}, u32[]{:S(2)}, u32[]{:S(2)}) %collective-permute-start.2) | collective-permute-done | bytes 131104 | tf_op jit(solution)/shard_map/ppermute | solution.py:224
  66.8 0.0 collective-permute-done.5
  66.8 0.1 broadcast_select_fusion.1
  66.8 1.3 %collective-permute-start.10 = (f32[1024,128]{1,0:T(8,128)S(1)}, f32[1024,128]{1,0:T(8,128)S(1)}, u32[]{:S(2)}, u32[]{:S(2)}) collective-permute-start(f32[1024,128]{1,0:T(8,128)S(1)} %broadcast_select_fusion.1), channel_id=1, source_target_pairs={{0,2},{1,31},{4,6},{5,3},{8,10},{9,7},{12,14},{13,11},{16,18},{17,... | collective-permute-start | bytes 1572872 | tf_op jit(solution)/shard_map/ppermute | solution.py:208
  68.2 1.3 %collective-permute-start.8 = (f32[16,2,8,128]{3,2,1,0:T(8,128)S(1)}, f32[16,2,8,128]{3,2,1,0:T(8,128)S(1)}, u32[]{:S(2)}, u32[]{:S(2)}) collective-permute-start(f32[16,2,8,128]{3,2,1,0:T(8,128)S(1)} %select_select_fusion.1), channel_id=1, source_target_pairs={{0,4},{1,29},{8,12},{9,5},{16,20},{17,13},{24,28},{25,21},{32,36},... | collective-permute-start | bytes 393224 | tf_op jit(solution)/shard_map/ppermute | solution.py:224
  69.5 1.3 %collective-permute-start.7 = (f32[16,2,8,128]{3,2,1,0:T(8,128)S(1)}, f32[16,2,8,128]{3,2,1,0:T(8,128)S(1)}, u32[]{:S(2)}, u32[]{:S(2)}) collective-permute-start(f32[16,2,8,128]{3,2,1,0:T(8,128)S(1)} %select_select_fusion.1), channel_id=1, source_target_pairs={{0,6},{1,27},{8,14},{9,3},{16,22},{17,11},{24,30},{25,19},{32,38},... | collective-permute-start | bytes 393224 | tf_op jit(solution)/shard_map/ppermute | solution.py:224
  70.8 1.3 %collective-permute-start.6 = (f32[16,2,8,128]{3,2,1,0:T(8,128)S(1)}, f32[16,2,8,128]{3,2,1,0:T(8,128)S(1)}, u32[]{:S(2)}, u32[]{:S(2)}) collective-permute-start(f32[16,2,8,128]{3,2,1,0:T(8,128)S(1)} %select_select_fusion.1), channel_id=1, source_target_pairs={{0,2},{1,31},{8,10},{9,7},{16,18},{17,15},{24,26},{25,23},{32,34},... | collective-permute-start | bytes 393224 | tf_op jit(solution)/shard_map/ppermute | solution.py:224
  72.1 3.6 %collective-permute-done.8 = f32[16,2,8,128]{3,2,1,0:T(8,128)S(1)} collective-permute-done((f32[16,2,8,128]{3,2,1,0:T(8,128)S(1)}, f32[16,2,8,128]{3,2,1,0:T(8,128)S(1)}, u32[]{:S(2)}, u32[]{:S(2)}) %collective-permute-start.8) | collective-permute-done | bytes 131104 | tf_op jit(solution)/shard_map/ppermute | solution.py:224
  75.7 1.4 %collective-permute-done.7 = f32[16,2,8,128]{3,2,1,0:T(8,128)S(1)} collective-permute-done((f32[16,2,8,128]{3,2,1,0:T(8,128)S(1)}, f32[16,2,8,128]{3,2,1,0:T(8,128)S(1)}, u32[]{:S(2)}, u32[]{:S(2)}) %collective-permute-start.7) | collective-permute-done | bytes 131104 | tf_op jit(solution)/shard_map/ppermute | solution.py:224
  77.1 1.4 %collective-permute-done.6 = f32[16,2,8,128]{3,2,1,0:T(8,128)S(1)} collective-permute-done((f32[16,2,8,128]{3,2,1,0:T(8,128)S(1)}, f32[16,2,8,128]{3,2,1,0:T(8,128)S(1)}, u32[]{:S(2)}, u32[]{:S(2)}) %collective-permute-start.6) | collective-permute-done | bytes 131104 | tf_op jit(solution)/shard_map/ppermute | solution.py:224
  78.5 0.0 copy-done
  78.5 0.0 copy-start.3
  78.5 5.9 %collective-permute-start.9 = (f32[16,2,8,128]{3,2,1,0:T(8,128)S(1)}, f32[16,2,8,128]{3,2,1,0:T(8,128)S(1)}, u32[]{:S(2)}, u32[]{:S(2)}) collective-permute-start(f32[16,2,8,128]{3,2,1,0:T(8,128)S(1)} %select_select_fusion.own), channel_id=1, source_target_pairs={{0,1},{1,0},{2,3},{3,2},{4,5},{5,4},{6,7},{7,6},{8,9},{9,8},{10,11... | collective-permute-start | bytes 393224 | tf_op jit(solution)/shard_map/ppermute | solution.py:195
  84.5 0.9 collective-permute-done.9.other
  85.4 0.0 copy-start.4
  85.4 0.0 collective-permute-done.10
  85.4 0.1 broadcast_select_fusion.own
  85.5 0.0 copy-start.1
  85.5 2.3 %collective-permute-start.11 = (f32[1024,128]{1,0:T(8,128)S(1)}, f32[1024,128]{1,0:T(8,128)S(1)}, u32[]{:S(2)}, u32[]{:S(2)}) collective-permute-start(f32[1024,128]{1,0:T(8,128)S(1)} %broadcast_select_fusion.own), channel_id=1, source_target_pairs={{0,1},{1,0},{2,3},{3,2},{4,5},{5,4},{6,7},{7,6},{8,9},{9,8},{10,11... | collective-permute-start | bytes 1572872 | tf_op jit(solution)/shard_map/ppermute | solution.py:195
  87.8 0.7 pad_add_fusion.place
  88.5 0.0 copy-done.3
  88.5 0.0 copy-done.4
  88.5 11.9 %factorise.1 = (f32[256,256]{1,0:T(8,128)}, f32[128,128]{1,0:T(8,128)}, f32[128,128]{1,0:T(8,128)}, f32[128,128]{1,0:T(8,128)}) custom-call(s32[2]{0:T(128)} %pad_add_fusion.place, f32[16,2,8,128]{3,2,1,0:T(8,128)} %copy-done.3, f32[16,2,8,128]{3,2,1,0:T(8,128)} %copy-done.4), custom_call_target="tpu_custom_call" | custom-call | tf_op jit(solution)/shard_map/factorise/pallas_call | solution.py:121
  100.3 0.0 collective-permute-done.11.other
  100.3 0.0 copy-start.2
  100.3 0.0 copy-done.1
  100.3 0.8 copy-done.2
  101.1 8.5 %update.1 = f32[4096,128]{1,0:T(8,128)} custom-call(s32[2]{0:T(128)} %pad_add_fusion.place, f32[256,256]{1,0:T(8,128)} %get-tuple-element.42.inv, f32[128,128]{1,0:T(8,128)} %get-tuple-element.43.l11, f32[128,128]{1,0:T(8,128)} %get-tuple-element.44.l21, f32[128,128]{1,0:T(8,128)} %get-tuple-element.45.l22, f32[1024,128]{1,0:T(8,128)} %copy-done.1, ...), custom_call_target="tpu_custom_call" | custom-call | tf_op jit(solution)/shard_map/update/pallas_call | solution.py:175
  (4 shorter events, 0.1 us)
Async XLA Ops:
  1.9 32.4 %collective-permute-start = (f32[1024,128]{1,0:T(8,128)S(1)}, f32[1024,128]{1,0:T(8,128)S(1)}, u32[]{:S(2)}, u32[]{:S(2)}) collective-permute-start(f32[1024,128]{1,0:T(8,128)S(1)} %slice_bitcast_fusion), channel_id=1, source_target_pairs={{0,16},{1,17},{32,48},{33,49},{64,80},{65,81},{96,112},{97,113},{1... | collective-permute-start | bytes 1572872 | tf_op jit(solution)/shard_map/ppermute | solution.py:208
  19.9 14.4 %all-to-all-start = ((f32[16,32,128]{2,1,0:T(8,128)}), f32[16,32,128]{2,1,0:T(8,128)S(1)}, u32[]{:S(2)}, u32[]{:S(2)}) async-start(f32[16,32,128]{2,1,0:T(8,128)} %bitcast.2), calls=%async_computation | async-start | bytes 524288 | tf_op jit(solution)/shard_map/all_to_all | solution.py:214
  35.2 14.6 %collective-permute-start.1 = (f32[1024,128]{1,0:T(8,128)S(1)}, f32[1024,128]{1,0:T(8,128)S(1)}, u32[]{:S(2)}, u32[]{:S(2)}) collective-permute-start(f32[1024,128]{1,0:T(8,128)S(1)} %broadcast_select_fusion.3), channel_id=1, source_target_pairs={{0,8},{1,25},{16,24},{17,9},{32,40},{33,57},{48,56},{49,41},{64,72... | collective-permute-start | bytes 1572872 | tf_op jit(solution)/shard_map/ppermute | solution.py:208
  36.5 13.0 %all-to-all-start.1 = ((f32[16,2,32,128]{3,2,1,0:T(8,128)}), f32[16,2,32,128]{3,2,1,0:T(8,128)S(1)}, u32[]{:S(2)}, u32[]{:S(2)}) async-start(f32[16,2,32,128]{3,2,1,0:T(8,128)} %broadcast_in_dim.2), calls=%async_computation.1 | async-start | bytes 1048576 | tf_op jit(solution)/shard_map/all_to_all | solution.py:218
  49.6 28.9 %copy-start = (f32[16,2,32,128]{3,2,1,0:T(8,128)}, f32[16,2,32,128]{3,2,1,0:T(8,128)S(1)}, u32[]{:S(2)}) copy-start(f32[16,2,32,128]{3,2,1,0:T(8,128)S(1)} %all-to-all-done.1.strips) | copy-start | bytes 1572868
  49.9 16.9 %collective-permute-start.5 = (f32[1024,128]{1,0:T(8,128)S(1)}, f32[1024,128]{1,0:T(8,128)S(1)}, u32[]{:S(2)}, u32[]{:S(2)}) collective-permute-start(f32[1024,128]{1,0:T(8,128)S(1)} %broadcast_select_fusion.2), channel_id=1, source_target_pairs={{0,4},{1,29},{8,12},{9,5},{16,20},{17,13},{24,28},{25,21},{32,36},... | collective-permute-start | bytes 1572872 | tf_op jit(solution)/shard_map/ppermute | solution.py:208
  51.2 13.6 %collective-permute-start.4 = (f32[16,2,8,128]{3,2,1,0:T(8,128)S(1)}, f32[16,2,8,128]{3,2,1,0:T(8,128)S(1)}, u32[]{:S(2)}, u32[]{:S(2)}) collective-permute-start(f32[16,2,8,128]{3,2,1,0:T(8,128)S(1)} %slice.16), channel_id=1, source_target_pairs={{0,16},{1,17},{32,48},{33,49},{64,80},{65,81},{96,112},{97,113},{1... | collective-permute-start | bytes 393224 | tf_op jit(solution)/shard_map/ppermute | solution.py:224
  62.2 3.3 %collective-permute-start.3 = (f32[16,2,8,128]{3,2,1,0:T(8,128)S(1)}, f32[16,2,8,128]{3,2,1,0:T(8,128)S(1)}, u32[]{:S(2)}, u32[]{:S(2)}) collective-permute-start(f32[16,2,8,128]{3,2,1,0:T(8,128)S(1)} %slice.16), channel_id=1, source_target_pairs={{0,24},{1,9},{32,56},{33,41},{64,88},{65,73},{96,120},{97,105},{12... | collective-permute-start | bytes 393224 | tf_op jit(solution)/shard_map/ppermute | solution.py:224
  63.5 3.2 %collective-permute-start.2 = (f32[16,2,8,128]{3,2,1,0:T(8,128)S(1)}, f32[16,2,8,128]{3,2,1,0:T(8,128)S(1)}, u32[]{:S(2)}, u32[]{:S(2)}) collective-permute-start(f32[16,2,8,128]{3,2,1,0:T(8,128)S(1)} %slice.16), channel_id=1, source_target_pairs={{0,8},{1,25},{32,40},{33,57},{64,72},{65,89},{96,104},{97,121},{12... | collective-permute-start | bytes 393224 | tf_op jit(solution)/shard_map/ppermute | solution.py:224
  66.8 18.6 %collective-permute-start.10 = (f32[1024,128]{1,0:T(8,128)S(1)}, f32[1024,128]{1,0:T(8,128)S(1)}, u32[]{:S(2)}, u32[]{:S(2)}) collective-permute-start(f32[1024,128]{1,0:T(8,128)S(1)} %broadcast_select_fusion.1), channel_id=1, source_target_pairs={{0,2},{1,31},{4,6},{5,3},{8,10},{9,7},{12,14},{13,11},{16,18},{17,... | collective-permute-start | bytes 1572872 | tf_op jit(solution)/shard_map/ppermute | solution.py:208
  68.2 7.5 %collective-permute-start.8 = (f32[16,2,8,128]{3,2,1,0:T(8,128)S(1)}, f32[16,2,8,128]{3,2,1,0:T(8,128)S(1)}, u32[]{:S(2)}, u32[]{:S(2)}) collective-permute-start(f32[16,2,8,128]{3,2,1,0:T(8,128)S(1)} %select_select_fusion.1), channel_id=1, source_target_pairs={{0,4},{1,29},{8,12},{9,5},{16,20},{17,13},{24,28},{25,21},{32,36},... | collective-permute-start | bytes 393224 | tf_op jit(solution)/shard_map/ppermute | solution.py:224
  69.5 7.6 %collective-permute-start.7 = (f32[16,2,8,128]{3,2,1,0:T(8,128)S(1)}, f32[16,2,8,128]{3,2,1,0:T(8,128)S(1)}, u32[]{:S(2)}, u32[]{:S(2)}) collective-permute-start(f32[16,2,8,128]{3,2,1,0:T(8,128)S(1)} %select_select_fusion.1), channel_id=1, source_target_pairs={{0,6},{1,27},{8,14},{9,3},{16,22},{17,11},{24,30},{25,19},{32,38},... | collective-permute-start | bytes 393224 | tf_op jit(solution)/shard_map/ppermute | solution.py:224
  70.8 7.7 %collective-permute-start.6 = (f32[16,2,8,128]{3,2,1,0:T(8,128)S(1)}, f32[16,2,8,128]{3,2,1,0:T(8,128)S(1)}, u32[]{:S(2)}, u32[]{:S(2)}) collective-permute-start(f32[16,2,8,128]{3,2,1,0:T(8,128)S(1)} %select_select_fusion.1), channel_id=1, source_target_pairs={{0,2},{1,31},{8,10},{9,7},{16,18},{17,15},{24,26},{25,23},{32,34},... | collective-permute-start | bytes 393224 | tf_op jit(solution)/shard_map/ppermute | solution.py:224
  78.5 10.0 %copy-start.3 = (f32[16,2,8,128]{3,2,1,0:T(8,128)}, f32[16,2,8,128]{3,2,1,0:T(8,128)S(1)}, u32[]{:S(2)}) copy-start(f32[16,2,8,128]{3,2,1,0:T(8,128)S(1)} %select_select_fusion.own) | copy-start | bytes 393220
  78.5 6.9 %collective-permute-start.9 = (f32[16,2,8,128]{3,2,1,0:T(8,128)S(1)}, f32[16,2,8,128]{3,2,1,0:T(8,128)S(1)}, u32[]{:S(2)}, u32[]{:S(2)}) collective-permute-start(f32[16,2,8,128]{3,2,1,0:T(8,128)S(1)} %select_select_fusion.own), channel_id=1, source_target_pairs={{0,1},{1,0},{2,3},{3,2},{4,5},{5,4},{6,7},{7,6},{8,9},{9,8},{10,11... | collective-permute-start | bytes 393224 | tf_op jit(solution)/shard_map/ppermute | solution.py:195
  85.4 3.0 %copy-start.4 = (f32[16,2,8,128]{3,2,1,0:T(8,128)}, f32[16,2,8,128]{3,2,1,0:T(8,128)S(1)}, u32[]{:S(2)}) copy-start(f32[16,2,8,128]{3,2,1,0:T(8,128)S(1)} %collective-permute-done.9.other) | copy-start | bytes 393220
  85.5 14.8 %copy-start.1 = (f32[1024,128]{1,0:T(8,128)}, f32[1024,128]{1,0:T(8,128)S(1)}, u32[]{:S(2)}) copy-start(f32[1024,128]{1,0:T(8,128)S(1)} %broadcast_select_fusion.own) | copy-start | bytes 1572868
  85.5 14.8 %collective-permute-start.11 = (f32[1024,128]{1,0:T(8,128)S(1)}, f32[1024,128]{1,0:T(8,128)S(1)}, u32[]{:S(2)}, u32[]{:S(2)}) collective-permute-start(f32[1024,128]{1,0:T(8,128)S(1)} %broadcast_select_fusion.own), channel_id=1, source_target_pairs={{0,1},{1,0},{2,3},{3,2},{4,5},{5,4},{6,7},{7,6},{8,9},{9,8},{10,11... | collective-permute-start | bytes 1572872 | tf_op jit(solution)/shard_map/ppermute | solution.py:195
  100.3 0.8 copy-start.2

commit v2 on v1

v2 whole, which is shorter than its diff:
```python
import jax
import jax.numpy as jnp
from jax import lax
from jax.experimental import pallas as pl
from jax.experimental.pallas import tpu as pltpu
from jax.sharding import PartitionSpec as P

HIGHEST = lax.Precision.HIGHEST
ROWS = 16
COLS = 32
LAYERS = 16
SIDE = 4
NB = 128
HALF = 64
PIECE = 8
CHUNKS = 2


def mm(a, b):
    return lax.dot_general(
        a, b, (((1,), (0,)), ((), ())), precision=HIGHEST, preferred_element_type=jnp.float32
    )


def mmt(a, b):
    return lax.dot_general(
        a, b, (((1,), (1,)), ((), ())), precision=HIGHEST, preferred_element_type=jnp.float32
    )


def split(a):
    high = a.astype(jnp.bfloat16)
    return high, (a - high.astype(jnp.float32)).astype(jnp.bfloat16)


def mm3(a, b):
    ah, al = split(a)
    bh, bl = b
    dot = lambda x, y: lax.dot_general(x, y, (((1,), (0,)), ((), ())), preferred_element_type=jnp.float32)
    return dot(ah, bh) + (dot(ah, bl) + dot(al, bh))


def eliminate(block, work):
    n = HALF
    shape = (8, 2 * n)
    lane = lax.broadcasted_iota(jnp.int32, shape, 1)
    sub = lax.broadcasted_iota(jnp.int32, shape, 0)
    work[:, :n] = block
    parts = []
    for i in range(n // 8):
        unit = jnp.where(lane == n + 8 * i + sub, 1.0, 0.0)
        parts.append(jnp.where(lane < n, work[8 * i : 8 * i + 8, :], unit))
    out = []
    for a in range(n // 8):
        rest = range(a + 1, n // 8)
        cols = []
        for j in range(8):
            k = 8 * a + j
            cols.append(
                {i: jnp.broadcast_to(parts[i][:, k : k + 1], shape) for i in range(a, n // 8)}
            )
        e = [
            [jnp.broadcast_to(cols[j][a][i : i + 1, :], shape) for j in range(i + 1)]
            for i in range(8)
        ]
        rows = [jnp.broadcast_to(parts[a][k : k + 1, :], shape) for k in range(8)]
        strip = None
        for k in range(8):
            inv = 1.0 / e[k][k]
            for i in range(k + 1, 8):
                low = e[i][k] * inv
                for j in range(k + 1, i + 1):
                    e[i][j] = e[i][j] - low * e[j][k]
                rows[i] = rows[i] - low * rows[k]
            root = lax.rsqrt(e[k][k])
            root = root * (1.5 - 0.5 * e[k][k] * root * root)
            done = rows[k] * root
            strip = done if k == 0 else jnp.where(sub == k, done, strip)
            for i in rest:
                m = cols[k][i] * inv
                for j in range(k + 1, 8):
                    cols[j][i] = cols[j][i] - m * e[j][k]
                parts[i] = parts[i] - m * rows[k]
        out.append(strip)
    full = jnp.concatenate(out, axis=0)
    r = lax.broadcasted_iota(jnp.int32, (n, n), 0)
    c = lax.broadcasted_iota(jnp.int32, (n, n), 1)
    return jnp.where(r <= c, full[:, :n], 0.0), jnp.where(r >= c, full[:, n:], 0.0)


def factor_block(s, work, upper):
    h = HALF
    u11, i11 = eliminate(s[:h, :h], work)
    l21 = mmt(s[h:, :h], i11)
    t21 = mm(l21, i11)
    u22, i22 = eliminate(s[h:, h:] - mmt(l21, l21), work)
    upper[:h, :h] = u11
    upper[:h, h:] = l21.T
    upper[h:, :h] = jnp.zeros((h, h), jnp.float32)
    upper[h:, h:] = u22
    return i11, -mm(i22, t21), i22


def factor_kernel(col, own, other, packed, l11, l21, l22, work, upper, inv):
    h, n = HALF, NB
    even = col[0] == 0

    def block(side, half):
        a, b = own[half], other[half]
        return jnp.where(even, a, b) if side == 0 else jnp.where(even, b, a)

    def put(to, blocks):
        to[:h, :h] = blocks[0]
        to[:h, h:] = jnp.zeros((h, h), jnp.float32)
        to[h:, :h] = blocks[1]
        to[h:, h:] = blocks[2]

    @pl.when(col[0] < 2)
    def _():
        put(inv.at[0], factor_block(block(0, 0), work, upper))
        l11[...] = upper[...].T
        i11 = inv[0]
        p = mmt(block(0, 1), i11)
        t = mm(p, i11)
        l21[...] = p
        put(inv.at[1], factor_block(block(1, 1) - mmt(p, p), work, upper))
        l22[...] = upper[...].T
        i22 = inv[1]
        r = lax.broadcasted_iota(jnp.int32, (n, n), 0)
        c = lax.broadcasted_iota(jnp.int32, (n, n), 1)
        packed[:n] = jnp.where(r >= c, i11, i22.T)
        packed[n : 2 * n] = -mm(i22, t)
        diagonal = jnp.sum(jnp.where(r == c, i22, 0.0), axis=0, keepdims=True)
        packed[2 * n :] = jnp.broadcast_to(diagonal, (8, n))


def factorise(col, own, other):
    block = jax.ShapeDtypeStruct((NB, NB), jnp.float32)
    vmem = pl.BlockSpec(memory_space=pltpu.VMEM)
    return pl.pallas_call(
        factor_kernel,
        in_specs=[pl.BlockSpec(memory_space=pltpu.SMEM), vmem, vmem],
        out_specs=[vmem] * 4,
        out_shape=[jax.ShapeDtypeStruct((2 * NB + 8, NB), jnp.float32), block, block, block],
        scratch_shapes=[
            pltpu.VMEM((HALF, NB), jnp.float32),
            pltpu.VMEM((NB, NB), jnp.float32),
            pltpu.VMEM((2, NB, NB), jnp.float32),
        ],
        name="factorise",
    )(col, own, other)


def is_top(row):
    x = row % SIDE
    return (x == 0) | (x == SIDE - 1)


def update_kernel(at_row, at_col, held, two, one, three, l11, l21, l22, own, other, here, there, store, out, data, sems, outs):
    n = NB
    chunks = data.shape[0]
    rows_of = data.shape[1]
    loads = [pltpu.make_async_copy(store.at[pl.ds(i * rows_of, rows_of)], data.at[i], sems.at[i]) for i in range(chunks)]
    saves = [pltpu.make_async_copy(data.at[i], out.at[pl.ds(i * rows_of, rows_of)], outs.at[i]) for i in range(chunks)]
    for load in loads:
        load.start()
    row, col = at_row[0], at_col[0]
    even = col % 2 == 0
    top = is_top(row)
    halves = [[], []]
    for j in range(4):
        a = here[pl.ds(j, n, stride=4), :]
        b = there[pl.ds(j, n, stride=4), :]
        halves[0].append(jnp.where(top, a, b))
        halves[1].append(jnp.where(top, b, a))
    whole = jnp.concatenate([jnp.concatenate(h, axis=1) for h in halves], axis=0)
    r = lax.broadcasted_iota(jnp.int32, (n, n), 0)
    c = lax.broadcasted_iota(jnp.int32, (n, n), 1)
    core, z = col % 2, col // 2
    step = jnp.where(core == 0, z, LAYERS - z) % 4
    packed = jnp.where(step == 2, two[...], held[...])
    packed = jnp.where(step == 1, one[...], jnp.where(step == 3, three[...], packed))
    shared = packed[:n]
    i11 = jnp.where(r >= c, shared, 0.0)
    diagonal = jnp.where(r == c, packed[2 * n : 2 * n + 1], 0.0)
    i22 = jnp.where(r > c, shared.T, diagonal)
    inverse = jnp.concatenate(
        [
            jnp.concatenate([i11, jnp.zeros((n, n), jnp.float32)], axis=1),
            jnp.concatenate([packed[n : 2 * n], i22], axis=1),
        ],
        axis=0,
    )
    mirrored = split(mm(inverse, whole))
    count = rows_of // 4
    local = lax.broadcasted_iota(jnp.int32, (count, n), 0)
    lane = lax.broadcasted_iota(jnp.int32, (count, n), 1)
    for i in range(chunks):
        span = pl.ds(i * count, count)
        a, b = own[span, :], other[span, :]
        left, right = jnp.where(even, a, b), jnp.where(even, b, a)
        panel = mmt(jnp.concatenate([left, right], axis=1), inverse)
        update = mm3(panel, mirrored)
        grow = (i * (count // n) + local // n) * ROWS + row
        rid = grow * n + local % n
        loads[i].wait()
        for j in range(4):
            cid = (j * COLS + col) * n + lane
            rows = pl.ds(j, count, stride=4)
            kept = data[i, rows, :] - update[:, j * n : (j + 1) * n]
            data[i, rows, :] = jnp.where(rid >= cid, kept, 0.0)

        @pl.when(col < 2)
        def _():
            solved = jnp.where(col == 0, panel[:, :n], panel[:, n:])
            if i == 0:
                first = jnp.where(col == 0, l11[...], 0.0)
                second = jnp.where(col == 0, l21[...], l22[...])
                solved = jnp.where(grow == 0, jnp.tile(first, (count // n, 1)), solved)
                solved = jnp.where(grow == 1, jnp.tile(second, (count // n, 1)), solved)
            data[i, pl.ds(0, count, stride=4), :] = jnp.where(rid >= col * n + lane, solved, 0.0)

        saves[i].start()
    for save in saves:
        save.wait()


def update(row, col, inverse, l11, l21, l22, own, other, here, there, view):
    vmem = pl.BlockSpec(memory_space=pltpu.VMEM)
    smem = pl.BlockSpec(memory_space=pltpu.SMEM)
    anywhere = pl.BlockSpec(memory_space=pl.ANY)
    return pl.pallas_call(
        update_kernel,
        in_specs=[smem] * 2 + [vmem] * 11 + [anywhere],
        out_specs=anywhere,
        out_shape=jax.ShapeDtypeStruct(view.shape, jnp.float32),
        scratch_shapes=[
            pltpu.VMEM((CHUNKS, view.shape[0] // CHUNKS, NB), jnp.float32),
            pltpu.SemaphoreType.DMA((CHUNKS,)),
            pltpu.SemaphoreType.DMA((CHUNKS,)),
        ],
        name="update",
    )(row, col, *inverse, l11, l21, l22, own, other, here, there, view)


def z_pairs(root, held, stride):
    pairs = []
    for layer in held:
        for core, sign in ((0, 1), (1, -1)):
            a = (root + sign * layer) % LAYERS
            b = (root + sign * (layer + stride)) % LAYERS
            if root == 0 or b > 0:
                pairs.append((2 * a + core, 2 * b + core))
    return pairs


def plane_pairs(first, second):
    pairs = []
    for core, rows in ((0, first), (1, second)):
        for z in range(LAYERS):
            pairs += [(a * COLS + 2 * z + core, b * COLS + 2 * z + core) for a, b in rows]
    return pairs


def shards(matrix):
    row = lax.axis_index("row")
    col = lax.axis_index("col")
    at_row, at_col = row.reshape(1), col.reshape(1)
    core, z = col % 2, col // 2
    layer = jnp.where(core == 0, z, (LAYERS - z) % LAYERS)
    after = jnp.where(core == 0, (z + LAYERS - 1) % LAYERS, (LAYERS + 1 - z) % LAYERS)
    x, y = row % SIDE, row // SIDE
    view = matrix.reshape(-1, NB)

    def tie(*values):
        return lax.optimization_barrier(values)

    def send(value, pairs):
        return lax.ppermute(value, "col", pairs)

    def send_plane(value, first, second):
        return lax.ppermute(value, ("row", "col"), plane_pairs(first, second))

    def choose(step, held, parts):
        kept = jnp.where(step == 2, parts[0], held)
        return jnp.where(step == 1, parts[1], jnp.where(step == 3, parts[2], kept))

    across = lambda ys: [(SIDE * q + a, SIDE * q + b) for q in ys for a, b in ((0, 3), (1, 2))]
    along = lambda ys, by, xs: [(SIDE * q + i, SIDE * (q + by) + i) for q in ys for i in xs]
    strip, view = tie(view[: 4 * NB], view)
    moved = send_plane(strip, across([0]), along([0], 2, (0, 1)))
    column = view.reshape(-1, 4, NB)[:, 0, :]
    sent = send(column, [(0, 2), (1, 3)])
    strip = jnp.where(jnp.where(core == 0, x >= 2, y == 2), moved, strip)
    moved = send_plane(strip, along([0], 2, range(4)), along([0, 2], 1, (0, 1)))
    strip = jnp.where(jnp.where(core == 0, y == 2, y % 2 == 1), moved, strip)
    moved = send_plane(strip, along([0, 2], 1, range(4)), across(range(4)))
    _, sent, column = tie(strip, sent, column)
    column = jnp.where(z == 1, sent, column)
    sent = send(column, z_pairs(1, [0], 4))
    strip = jnp.where(jnp.where(core == 0, y % 2 == 1, x >= 2), moved, strip)
    swap = [(i, i ^ 1) for i in range(ROWS)]
    mine = strip[::4]
    theirs = send_plane(mine, swap, swap)
    _, sent, column = tie(strip, sent, column)
    column = jnp.where((z != 0) & (after == 4), sent, column)
    sent = send(column, z_pairs(1, [0], 12) + z_pairs(1, [4], 4))
    column = jnp.where((z != 0) & ((after == 8) | (after == 12)), sent, column)
    sent = send(column, z_pairs(1, range(0, 16, 4), 2))

    strip, theirs = tie(strip, theirs)
    facing = send_plane(strip, swap, swap)
    top = is_top(row)
    corner = jnp.stack([jnp.where(top, mine, theirs), jnp.where(top, theirs, mine)])
    other = send(corner, [(0, 1), (1, 0)])
    _, sent, column = tie(other, sent, column)
    column = jnp.where((z != 0) & (after % 4 == 2), sent, column)
    sent = send(column, z_pairs(1, range(0, 16, 2), 1))
    corner, other, column = tie(corner, other, column)
    inv, l11, l21, l22 = factorise(at_col, corner, other)
    inv, facing = tie(inv, facing)

    parts = [send(inv, z_pairs(0, [0], 4 * q)) for q in (2, 1, 3)]
    *parts, column = tie(*parts, column)
    inv = choose(layer // 4, inv, parts)
    _, sent, column = tie(inv, sent, column)
    parts = [send(inv, z_pairs(0, [0, 4, 8, 12], q)) for q in (2, 1, 3)]
    parts[0], sent, column = tie(parts[0], sent, column)
    column = jnp.where((z != 0) & (after % 2 == 1), sent, column)
    column_other = send(column, [(c, c ^ 1) for c in range(COLS)])
    *parts, column = tie(*parts, column)
    out = update(at_row, at_col, [inv, *parts], l11, l21, l22, column, column_other, strip, facing, view)
    return out.reshape(matrix.shape)


def solution(mesh):
    spec = P("row", None, None, "col", None, None)
    return jax.shard_map(shards, mesh=mesh, in_specs=(spec,), out_specs=spec, check_vma=False)
```

time: 110 us -> 87.2 us (0.79)
  the two profiles are of different devices: /device:TPU:1 before, /device:TPU:57 now
where the time goes in v2:
time: 87.2 us; the launch traced here: 86.6 us
  starting transfers between devices  42.5 us (49%)
  waiting for transfers between devices  29.4 us (34%)
  Pallas kernels  8.92 us (10%)
  local copies, waits for them, and re-layouts  3.82 us (4%)
  other arithmetic  1.35 us (2%)
    ppermute x13, starting transfers between devices, send(): return lax.ppermute(value, 'col', pairs)  33 us
    ppermute x13, waiting for transfers between devices, send(): return lax.ppermute(value, 'col', pairs)  17.1 us
    ppermute x5, waiting for transfers between devices, send_plane(): return lax.ppermute(value, ('row', 'col'), plane_pairs(first, second))  12.3 us
    ppermute x5, starting transfers between devices, send_plane(): return lax.ppermute(value, ('row', 'col'), plane_pairs(first, second))  9.51 us
    pallas_call x1, Pallas kernels, update(): pl.pallas_call(update_kernel, in_specs=[smem] * 2 + [vmem] * 11 + [anywhe...  7.23 us
    slice x1, local copies, waits for them, and re-layouts, shards(): column = view.reshape(-1, 4, NB)[:, 0, :]  1.95 us
  transfers between devices with their start and end apart: 18, of which 7 were waited for; matrix products, arithmetic and copies ran while one was open for 4% of the time, Pallas kernels for 2%

profile of v2, /device:TPU:57, one launch (start us, length us, event | category | flops | bytes accessed | tf_op | source)
XLA Modules:
  0.0 86.6 jit_solution(3669212293220424857)
XLA Ops:
  0.0 1.0 %slice.12 = f32[1,1,128,1,4,128]{5,4,3,2,1,0:T(4,128)S(1)} slice(f32[1,8,128,1,4,128]{5,4,3,2,1,0:T(4,128)} %param.1), slice={[0:1], [0:1], [0:128], [0:1], [0:4], [0:128]} | slice | bytes 524288 | tf_op jit(solution)/shard_map/slice | solution.py:290
  1.0 0.7 collective-permute-start
  1.7 2.0 %slice.16 = f32[1024,1,128]{2,1,0:T(1,128)S(1)} slice(f32[1024,4,128]{2,1,0:T(4,128)} %bitcast.15), slice={[0:1024], [0:1], [0:128]} | slice | bytes 1048576 | tf_op jit(solution)/shard_map/slice | solution.py:292
  3.6 1.3 %collective-permute-start.5 = (f32[1024,128]{1,0:T(8,128)S(1)}, f32[1024,128]{1,0:T(8,128)S(1)}, u32[]{:S(2)}, u32[]{:S(2)}) collective-permute-start(f32[1024,128]{1,0:T(8,128)S(1)} %bitcast.17), channel_id=1, source_target_pairs={{0,2},{1,3},{32,34},{33,35},{64,66},{65,67},{96,98},{97,99},{128,1... | collective-permute-start | bytes 1572872 | tf_op jit(solution)/shard_map/ppermute | solution.py:279
  5.0 0.0 collective-permute-done
  5.0 1.3 %collective-permute-start.1 = (f32[512,128]{1,0:T(8,128)S(1)}, f32[512,128]{1,0:T(8,128)S(1)}, u32[]{:S(2)}, u32[]{:S(2)}) collective-permute-start(f32[512,128]{1,0:T(8,128)S(1)} %broadcast_select_fusion.5), channel_id=1, source_target_pairs={{0,256},{32,288},{64,320},{96,352},{2,258},{34,290},{66,322},{98,3... | collective-permute-start | bytes 786440 | tf_op jit(solution)/shard_map/ppermute | solution.py:282
  6.3 9.1 %collective-permute-done.1 = f32[512,128]{1,0:T(8,128)S(1)} collective-permute-done((f32[512,128]{1,0:T(8,128)S(1)}, f32[512,128]{1,0:T(8,128)S(1)}, u32[]{:S(2)}, u32[]{:S(2)}) %collective-permute-start.1) | collective-permute-done | bytes 262176 | tf_op jit(solution)/shard_map/ppermute | solution.py:282
  15.5 2.8 %collective-permute-done.5 = f32[1024,128]{1,0:T(8,128)S(1)} collective-permute-done((f32[1024,128]{1,0:T(8,128)S(1)}, f32[1024,128]{1,0:T(8,128)S(1)}, u32[]{:S(2)}, u32[]{:S(2)}) %collective-permute-start.5) | collective-permute-done | bytes 524320 | tf_op jit(solution)/shard_map/ppermute | solution.py:279
  18.3 0.1 broadcast_select_fusion.1
  18.4 8.5 %collective-permute-start.6 = (f32[1024,128]{1,0:T(8,128)S(1)}, f32[1024,128]{1,0:T(8,128)S(1)}, u32[]{:S(2)}, u32[]{:S(2)}) collective-permute-start(f32[1024,128]{1,0:T(8,128)S(1)} %broadcast_select_fusion.1), channel_id=1, source_target_pairs={{2,10},{3,27},{34,42},{35,59},{66,74},{67,91},{98,106},{99,123},{1... | collective-permute-start | bytes 1572872 | tf_op jit(solution)/shard_map/ppermute | solution.py:279
  26.8 1.3 %collective-permute-start.2 = (f32[512,128]{1,0:T(8,128)S(1)}, f32[512,128]{1,0:T(8,128)S(1)}, u32[]{:S(2)}, u32[]{:S(2)}) collective-permute-start(f32[512,128]{1,0:T(8,128)S(1)} %broadcast_select_fusion.6), channel_id=1, source_target_pairs={{0,128},{32,160},{64,192},{96,224},{256,384},{288,416},{320,448},{... | collective-permute-start | bytes 786440 | tf_op jit(solution)/shard_map/ppermute | solution.py:282
  28.2 3.2 %collective-permute-done.2 = f32[512,128]{1,0:T(8,128)S(1)} collective-permute-done((f32[512,128]{1,0:T(8,128)S(1)}, f32[512,128]{1,0:T(8,128)S(1)}, u32[]{:S(2)}, u32[]{:S(2)}) %collective-permute-start.2) | collective-permute-done | bytes 262176 | tf_op jit(solution)/shard_map/ppermute | solution.py:282
  31.5 0.0 copy-start.1
  31.5 1.4 %collective-permute-done.6 = f32[1024,128]{1,0:T(8,128)S(1)} collective-permute-done((f32[1024,128]{1,0:T(8,128)S(1)}, f32[1024,128]{1,0:T(8,128)S(1)}, u32[]{:S(2)}, u32[]{:S(2)}) %collective-permute-start.6) | collective-permute-done | bytes 524320 | tf_op jit(solution)/shard_map/ppermute | solution.py:279
  32.9 0.1 broadcast_select_fusion.2
  33.0 1.3 %collective-permute-start.7 = (f32[1024,128]{1,0:T(8,128)S(1)}, f32[1024,128]{1,0:T(8,128)S(1)}, u32[]{:S(2)}, u32[]{:S(2)}) collective-permute-start(f32[1024,128]{1,0:T(8,128)S(1)} %broadcast_select_fusion.2), channel_id=1, source_target_pairs={{2,26},{3,11},{10,18},{27,19},{34,58},{35,43},{42,50},{59,51},{66,... | collective-permute-start | bytes 1572872 | tf_op jit(solution)/shard_map/ppermute | solution.py:279
  34.3 3.1 %collective-permute-start.3 = (f32[128,128]{1,0:T(8,128)S(1)}, f32[128,128]{1,0:T(8,128)S(1)}, u32[]{:S(2)}, u32[]{:S(2)}) collective-permute-start(f32[128,128]{1,0:T(8,128)S(1)} %slice.14), channel_id=1, source_target_pairs={{0,32},{32,0},{64,96},{96,64},{128,160},{160,128},{192,224},{224,1... | collective-permute-start | bytes 196616 | tf_op jit(solution)/shard_map/ppermute | solution.py:282
  37.5 2.9 %collective-permute-done.7 = f32[1024,128]{1,0:T(8,128)S(1)} collective-permute-done((f32[1024,128]{1,0:T(8,128)S(1)}, f32[1024,128]{1,0:T(8,128)S(1)}, u32[]{:S(2)}, u32[]{:S(2)}) %collective-permute-start.7) | collective-permute-done | bytes 524320 | tf_op jit(solution)/shard_map/ppermute | solution.py:279
  40.4 0.1 broadcast_select_fusion.3
  40.4 1.3 %collective-permute-start.8 = (f32[1024,128]{1,0:T(8,128)S(1)}, f32[1024,128]{1,0:T(8,128)S(1)}, u32[]{:S(2)}, u32[]{:S(2)}) collective-permute-start(f32[1024,128]{1,0:T(8,128)S(1)} %broadcast_select_fusion.3), channel_id=1, source_target_pairs={{2,6},{3,31},{10,14},{27,23},{18,22},{19,15},{26,30},{11,7},{34,38... | collective-permute-start | bytes 1572872 | tf_op jit(solution)/shard_map/ppermute | solution.py:279
  41.8 0.0 collective-permute-done.3
  41.8 0.0 copy-start.3
  41.8 0.7 collective-permute-start.4
  42.5 3.1 %collective-permute-start.9 = (f32[512,128]{1,0:T(8,128)S(1)}, f32[512,128]{1,0:T(8,128)S(1)}, u32[]{:S(2)}, u32[]{:S(2)}) collective-permute-start(f32[512,128]{1,0:T(8,128)S(1)} %broadcast_select_fusion.7.here), channel_id=1, source_target_pairs={{0,32},{32,0},{64,96},{96,64},{128,160},{160,128},{192,224},{224,1... | collective-permute-start | bytes 786440 | tf_op jit(solution)/shard_map/ppermute | solution.py:282
  45.7 0.0 collective-permute-done.4.other
  45.7 0.0 copy-start.9
  45.7 3.1 %collective-permute-done.8 = f32[1024,128]{1,0:T(8,128)S(1)} collective-permute-done((f32[1024,128]{1,0:T(8,128)S(1)}, f32[1024,128]{1,0:T(8,128)S(1)}, u32[]{:S(2)}, u32[]{:S(2)}) %collective-permute-start.8) | collective-permute-done | bytes 524320 | tf_op jit(solution)/shard_map/ppermute | solution.py:279
  48.8 0.1 broadcast_select_fusion.4
  48.8 0.0 copy-done.1
  48.8 0.7 collective-permute-start.14
  49.5 0.0 copy-done.3
  49.5 0.0 copy-done.9
  49.6 1.7 %factorise.1 = (f32[264,128]{1,0:T(8,128)}, f32[128,128]{1,0:T(8,128)}, f32[128,128]{1,0:T(8,128)}, f32[128,128]{1,0:T(8,128)}) custom-call(s32[1]{0:T(128)} %bitcast.1.col.at_col, f32[2,128,128]{2,1,0:T(8,128)} %copy-done.3, f32[2,128,128]{2,1,0:T(8,128)} %copy-done.9), custom_call_target="tpu_custom_call" | custom-call | tf_op jit(solution)/shard_map/factorise/pallas_call | solution.py:140
  51.2 0.0 collective-permute-done.9.there
  51.2 0.0 copy-start.5
  51.2 0.7 collective-permute-start.12
  51.9 0.7 collective-permute-start.11
  52.6 0.7 collective-permute-start.10
  53.3 0.0 collective-permute-done.12
  53.3 0.0 collective-permute-done.11
  53.3 0.0 collective-permute-done.10
  53.4 1.0 %select_select_fusion.held = f32[264,128]{1,0:T(8,128)S(1)} fusion(f32[264,128]{1,0:T(8,128)S(1)} %collective-permute-done.11, f32[264,128]{1,0:T(8,128)S(1)} %collective-permute-done.12, f32[264,128]{1,0:T(8,128)S(1)} %collective-permute-done.10, f32[264,128]{1,0:T(8,128)} %get-tuple-element.50, pred[]{:T(512)S(6)} %eq.71, pred[]{:T(512)S(6)} %eq.70, pred[]{:T(512)S(6)} %eq.60), kind=kLoop, calls=%fused_computation.5 | loop fusion | flops 101376 | bytes 675843 | tf_op jit(solution)/shard_map/jit(_where)/select_n | solution.py:286
  54.3 0.0 copy-start.2
  54.3 0.7 collective-permute-start.13
  55.0 0.0 collective-permute-done.14
  55.0 0.0 collective-permute-done.13.two
  55.0 0.0 copy-start.6
  55.1 0.1 broadcast_select_fusion.own
  55.1 0.0 copy-start
  55.1 14.6 %collective-permute-start.17 = (f32[1024,128]{1,0:T(8,128)S(1)}, f32[1024,128]{1,0:T(8,128)S(1)}, u32[]{:S(2)}, u32[]{:S(2)}) collective-permute-start(f32[1024,128]{1,0:T(8,128)S(1)} %broadcast_select_fusion.own), channel_id=1, source_target_pairs={{0,1},{1,0},{2,3},{3,2},{4,5},{5,4},{6,7},{7,6},{8,9},{9,8},{10,11... | collective-permute-start | bytes 1572872 | tf_op jit(solution)/shard_map/ppermute | solution.py:279
  69.7 1.3 %collective-permute-start.16 = (f32[264,128]{1,0:T(8,128)S(1)}, f32[264,128]{1,0:T(8,128)S(1)}, u32[]{:S(2)}, u32[]{:S(2)}) collective-permute-start(f32[264,128]{1,0:T(8,128)S(1)} %select_select_fusion.held), channel_id=1, source_target_pairs={{0,6},{1,27},{8,14},{25,19},{16,22},{17,11},{24,30},{9,3},{32,38},... | collective-permute-start | bytes 405512 | tf_op jit(solution)/shard_map/ppermute | solution.py:279
  71.0 0.7 collective-permute-start.15
  71.7 6.8 %collective-permute-done.16.three = f32[264,128]{1,0:T(8,128)S(1)} collective-permute-done((f32[264,128]{1,0:T(8,128)S(1)}, f32[264,128]{1,0:T(8,128)S(1)}, u32[]{:S(2)}, u32[]{:S(2)}) %collective-permute-start.16) | collective-permute-done | bytes 135200 | tf_op jit(solution)/shard_map/ppermute | solution.py:279
  78.5 0.0 collective-permute-done.15.one
  78.5 0.0 collective-permute-done.17.other
  78.5 0.0 copy-start.4
  78.5 0.0 copy-done.5
  78.5 0.0 copy-done.2
  78.5 0.0 copy-done.6
  78.5 0.0 copy-done
  78.6 0.6 copy-done.7
  79.2 0.0 copy-done.8
  79.2 0.2 copy-done.4
  79.4 7.2 %update.1 = f32[4096,128]{1,0:T(8,128)} custom-call(s32[1]{0:T(128)} %bitcast.at_row, s32[1]{0:T(128)} %bitcast.1.col.at_col, f32[264,128]{1,0:T(8,128)} %copy-done.2, f32[264,128]{1,0:T(8,128)} %copy-done.6, f32[264,128]{1,0:T(8,128)} %copy-done.8, f32[264,128]{1,0:T(8,128)} %copy-done.7, f32[128,128]{1,0:T(8,128)} %get-tuple-element.64.l11, ...), custom_call_target="tpu_custom_call" | custom-call | tf_op jit(solution)/shard_map/update/pallas_call | solution.py:232
  (8 shorter events, 0.1 us)
Async XLA Ops:
  1.0 4.0 %collective-permute-start = (f32[512,128]{1,0:T(8,128)S(1)}, f32[512,128]{1,0:T(8,128)S(1)}, u32[]{:S(2)}, u32[]{:S(2)}) collective-permute-start(f32[512,128]{1,0:T(8,128)S(1)} %bitcast.19), channel_id=1, source_target_pairs={{0,96},{32,64},{2,98},{34,66},{4,100},{36,68},{6,102},{38,70},{8,1... | collective-permute-start | bytes 786440 | tf_op jit(solution)/shard_map/ppermute | solution.py:282
  3.6 14.7 %collective-permute-start.5 = (f32[1024,128]{1,0:T(8,128)S(1)}, f32[1024,128]{1,0:T(8,128)S(1)}, u32[]{:S(2)}, u32[]{:S(2)}) collective-permute-start(f32[1024,128]{1,0:T(8,128)S(1)} %bitcast.17), channel_id=1, source_target_pairs={{0,2},{1,3},{32,34},{33,35},{64,66},{65,67},{96,98},{97,99},{128,1... | collective-permute-start | bytes 1572872 | tf_op jit(solution)/shard_map/ppermute | solution.py:279
  5.0 10.4 %collective-permute-start.1 = (f32[512,128]{1,0:T(8,128)S(1)}, f32[512,128]{1,0:T(8,128)S(1)}, u32[]{:S(2)}, u32[]{:S(2)}) collective-permute-start(f32[512,128]{1,0:T(8,128)S(1)} %broadcast_select_fusion.5), channel_id=1, source_target_pairs={{0,256},{32,288},{64,320},{96,352},{2,258},{34,290},{66,322},{98,3... | collective-permute-start | bytes 786440 | tf_op jit(solution)/shard_map/ppermute | solution.py:282
  18.4 14.5 %collective-permute-start.6 = (f32[1024,128]{1,0:T(8,128)S(1)}, f32[1024,128]{1,0:T(8,128)S(1)}, u32[]{:S(2)}, u32[]{:S(2)}) collective-permute-start(f32[1024,128]{1,0:T(8,128)S(1)} %broadcast_select_fusion.1), channel_id=1, source_target_pairs={{2,10},{3,27},{34,42},{35,59},{66,74},{67,91},{98,106},{99,123},{1... | collective-permute-start | bytes 1572872 | tf_op jit(solution)/shard_map/ppermute | solution.py:279
  26.8 4.6 %collective-permute-start.2 = (f32[512,128]{1,0:T(8,128)S(1)}, f32[512,128]{1,0:T(8,128)S(1)}, u32[]{:S(2)}, u32[]{:S(2)}) collective-permute-start(f32[512,128]{1,0:T(8,128)S(1)} %broadcast_select_fusion.6), channel_id=1, source_target_pairs={{0,128},{32,160},{64,192},{96,224},{256,384},{288,416},{320,448},{... | collective-permute-start | bytes 786440 | tf_op jit(solution)/shard_map/ppermute | solution.py:282
  31.5 17.4 %copy-start.1 = (f32[512,128]{1,0:T(8,128)}, f32[512,128]{1,0:T(8,128)S(1)}, u32[]{:S(2)}) copy-start(f32[512,128]{1,0:T(8,128)S(1)} %broadcast_select_fusion.7.here) | copy-start | bytes 786436
  33.0 7.4 %collective-permute-start.7 = (f32[1024,128]{1,0:T(8,128)S(1)}, f32[1024,128]{1,0:T(8,128)S(1)}, u32[]{:S(2)}, u32[]{:S(2)}) collective-permute-start(f32[1024,128]{1,0:T(8,128)S(1)} %broadcast_select_fusion.2), channel_id=1, source_target_pairs={{2,26},{3,11},{10,18},{27,19},{34,58},{35,43},{42,50},{59,51},{66,... | collective-permute-start | bytes 1572872 | tf_op jit(solution)/shard_map/ppermute | solution.py:279
  34.3 7.4 %collective-permute-start.3 = (f32[128,128]{1,0:T(8,128)S(1)}, f32[128,128]{1,0:T(8,128)S(1)}, u32[]{:S(2)}, u32[]{:S(2)}) collective-permute-start(f32[128,128]{1,0:T(8,128)S(1)} %slice.14), channel_id=1, source_target_pairs={{0,32},{32,0},{64,96},{96,64},{128,160},{160,128},{192,224},{224,1... | collective-permute-start | bytes 196616 | tf_op jit(solution)/shard_map/ppermute | solution.py:282
  40.4 8.3 %collective-permute-start.8 = (f32[1024,128]{1,0:T(8,128)S(1)}, f32[1024,128]{1,0:T(8,128)S(1)}, u32[]{:S(2)}, u32[]{:S(2)}) collective-permute-start(f32[1024,128]{1,0:T(8,128)S(1)} %broadcast_select_fusion.3), channel_id=1, source_target_pairs={{2,6},{3,31},{10,14},{27,23},{18,22},{19,15},{26,30},{11,7},{34,38... | collective-permute-start | bytes 1572872 | tf_op jit(solution)/shard_map/ppermute | solution.py:279
  41.8 7.7 %copy-start.3 = (f32[2,128,128]{2,1,0:T(8,128)}, f32[2,128,128]{2,1,0:T(8,128)S(1)}, u32[]{:S(2)}) copy-start(f32[2,128,128]{2,1,0:T(8,128)S(1)} %pad_maximum_fusion.own) | copy-start | bytes 393220
  41.8 3.8 %collective-permute-start.4 = (f32[2,128,128]{2,1,0:T(8,128)S(1)}, f32[2,128,128]{2,1,0:T(8,128)S(1)}, u32[]{:S(2)}, u32[]{:S(2)}) collective-permute-start(f32[2,128,128]{2,1,0:T(8,128)S(1)} %pad_maximum_fusion.own), channel_id=1, source_target_pairs={{0,1},{1,0},{32,33},{33,32},{64,65},{65,64},{96,97},{97,96},{128,1... | collective-permute-start | bytes 393224 | tf_op jit(solution)/shard_map/ppermute | solution.py:279
  42.5 8.7 %collective-permute-start.9 = (f32[512,128]{1,0:T(8,128)S(1)}, f32[512,128]{1,0:T(8,128)S(1)}, u32[]{:S(2)}, u32[]{:S(2)}) collective-permute-start(f32[512,128]{1,0:T(8,128)S(1)} %broadcast_select_fusion.7.here), channel_id=1, source_target_pairs={{0,32},{32,0},{64,96},{96,64},{128,160},{160,128},{192,224},{224,1... | collective-permute-start | bytes 786440 | tf_op jit(solution)/shard_map/ppermute | solution.py:282
  45.7 3.9 %copy-start.9 = (f32[2,128,128]{2,1,0:T(8,128)}, f32[2,128,128]{2,1,0:T(8,128)S(1)}, u32[]{:S(2)}) copy-start(f32[2,128,128]{2,1,0:T(8,128)S(1)} %collective-permute-done.4.other) | copy-start | bytes 393220
  48.8 6.2 %collective-permute-start.14 = (f32[1024,128]{1,0:T(8,128)S(1)}, f32[1024,128]{1,0:T(8,128)S(1)}, u32[]{:S(2)}, u32[]{:S(2)}) collective-permute-start(f32[1024,128]{1,0:T(8,128)S(1)} %broadcast_select_fusion.4), channel_id=1, source_target_pairs={{2,4},{6,8},{31,29},{10,12},{27,25},{14,16},{23,21},{18,20},{19,17... | collective-permute-start | bytes 1572872 | tf_op jit(solution)/shard_map/ppermute | solution.py:279
  51.2 27.3 %copy-start.5 = (f32[512,128]{1,0:T(8,128)}, f32[512,128]{1,0:T(8,128)S(1)}, u32[]{:S(2)}) copy-start(f32[512,128]{1,0:T(8,128)S(1)} %collective-permute-done.9.there) | copy-start | bytes 786436
  51.2 2.1 %collective-permute-start.12 = (f32[264,128]{1,0:T(8,128)}, f32[264,128]{1,0:T(8,128)S(1)}, u32[]{:S(2)}, u32[]{:S(2)}) collective-permute-start(f32[264,128]{1,0:T(8,128)} %get-tuple-element.50), channel_id=1, source_target_pairs={{0,24},{1,9},{32,56},{33,41},{64,88},{65,73},{96,120},{97,105},{12... | collective-permute-start | bytes 405512 | tf_op jit(solution)/shard_map/ppermute | solution.py:279
  51.9 1.4 %collective-permute-start.11 = (f32[264,128]{1,0:T(8,128)}, f32[264,128]{1,0:T(8,128)S(1)}, u32[]{:S(2)}, u32[]{:S(2)}) collective-permute-start(f32[264,128]{1,0:T(8,128)} %get-tuple-element.50), channel_id=1, source_target_pairs={{0,8},{1,25},{32,40},{33,57},{64,72},{65,89},{96,104},{97,121},{12... | collective-permute-start | bytes 405512 | tf_op jit(solution)/shard_map/ppermute | solution.py:279
  52.6 0.8 collective-permute-start.10
  54.3 24.2 %copy-start.2 = (f32[264,128]{1,0:T(8,128)}, f32[264,128]{1,0:T(8,128)S(1)}, u32[]{:S(2)}) copy-start(f32[264,128]{1,0:T(8,128)S(1)} %select_select_fusion.held) | copy-start | bytes 405508
  54.3 0.7 collective-permute-start.13
  55.0 23.5 %copy-start.6 = (f32[264,128]{1,0:T(8,128)}, f32[264,128]{1,0:T(8,128)S(1)}, u32[]{:S(2)}) copy-start(f32[264,128]{1,0:T(8,128)S(1)} %collective-permute-done.13.two) | copy-start | bytes 405508
  55.1 23.4 %copy-start = (f32[1024,128]{1,0:T(8,128)}, f32[1024,128]{1,0:T(8,128)S(1)}, u32[]{:S(2)}) copy-start(f32[1024,128]{1,0:T(8,128)S(1)} %broadcast_select_fusion.own) | copy-start | bytes 1572868
  55.1 23.4 %collective-permute-start.17 = (f32[1024,128]{1,0:T(8,128)S(1)}, f32[1024,128]{1,0:T(8,128)S(1)}, u32[]{:S(2)}, u32[]{:S(2)}) collective-permute-start(f32[1024,128]{1,0:T(8,128)S(1)} %broadcast_select_fusion.own), channel_id=1, source_target_pairs={{0,1},{1,0},{2,3},{3,2},{4,5},{5,4},{6,7},{7,6},{8,9},{9,8},{10,11... | collective-permute-start | bytes 1572872 | tf_op jit(solution)/shard_map/ppermute | solution.py:279
  69.7 8.8 %collective-permute-start.16 = (f32[264,128]{1,0:T(8,128)S(1)}, f32[264,128]{1,0:T(8,128)S(1)}, u32[]{:S(2)}, u32[]{:S(2)}) collective-permute-start(f32[264,128]{1,0:T(8,128)S(1)} %select_select_fusion.held), channel_id=1, source_target_pairs={{0,6},{1,27},{8,14},{25,19},{16,22},{17,11},{24,30},{9,3},{32,38},... | collective-permute-start | bytes 405512 | tf_op jit(solution)/shard_map/ppermute | solution.py:279
  71.0 7.5 %collective-permute-start.15 = (f32[264,128]{1,0:T(8,128)S(1)}, f32[264,128]{1,0:T(8,128)S(1)}, u32[]{:S(2)}, u32[]{:S(2)}) collective-permute-start(f32[264,128]{1,0:T(8,128)S(1)} %select_select_fusion.held), channel_id=1, source_target_pairs={{0,2},{1,31},{8,10},{25,23},{16,18},{17,15},{24,26},{9,7},{32,34},... | collective-permute-start | bytes 405512 | tf_op jit(solution)/shard_map/ppermute | solution.py:279
  78.5 0.7 copy-start.7
  78.5 0.7 copy-start.8
  78.5 0.9 %copy-start.4 = (f32[1024,128]{1,0:T(8,128)}, f32[1024,128]{1,0:T(8,128)S(1)}, u32[]{:S(2)}) copy-start(f32[1024,128]{1,0:T(8,128)S(1)} %collective-permute-done.17.other) | copy-start | bytes 1572868

commit v3 on v2

--- a/solution.py
+++ b/solution.py
@@ -296,16 +296,16 @@
     strip = jnp.where(jnp.where(core == 0, y == 2, y % 2 == 1), moved, strip)
     moved = send_plane(strip, along([0, 2], 1, range(4)), across(range(4)))
     _, sent, column = tie(strip, sent, column)
-    column = jnp.where(z == 1, sent, column)
+    panel, column = column, sent
     sent = send(column, z_pairs(1, [0], 4))
     strip = jnp.where(jnp.where(core == 0, y % 2 == 1, x >= 2), moved, strip)
     swap = [(i, i ^ 1) for i in range(ROWS)]
     mine = strip[::4]
     theirs = send_plane(mine, swap, swap)
     _, sent, column = tie(strip, sent, column)
-    column = jnp.where((z != 0) & (after == 4), sent, column)
+    column = jnp.where(after == 4, sent, column)
     sent = send(column, z_pairs(1, [0], 12) + z_pairs(1, [4], 4))
-    column = jnp.where((z != 0) & ((after == 8) | (after == 12)), sent, column)
+    column = jnp.where((after == 8) | (after == 12), sent, column)
     sent = send(column, z_pairs(1, range(0, 16, 4), 2))
 
     strip, theirs = tie(strip, theirs)
@@ -314,7 +314,7 @@
     corner = jnp.stack([jnp.where(top, mine, theirs), jnp.where(top, theirs, mine)])
     other = send(corner, [(0, 1), (1, 0)])
     _, sent, column = tie(other, sent, column)
-    column = jnp.where((z != 0) & (after % 4 == 2), sent, column)
+    column = jnp.where(after % 4 == 2, sent, column)
     sent = send(column, z_pairs(1, range(0, 16, 2), 1))
     corner, other, column = tie(corner, other, column)
     inv, l11, l21, l22 = factorise(at_col, corner, other)
@@ -325,8 +325,8 @@
     inv = choose(layer // 4, inv, parts)
     _, sent, column = tie(inv, sent, column)
     parts = [send(inv, z_pairs(0, [0, 4, 8, 12], q)) for q in (2, 1, 3)]
-    parts[0], sent, column = tie(parts[0], sent, column)
-    column = jnp.where((z != 0) & (after % 2 == 1), sent, column)
+    *parts, sent, column = tie(*parts, sent, column)
+    column = jnp.where(z == 0, panel, jnp.where(after % 2 == 1, sent, column))
     column_other = send(column, [(c, c ^ 1) for c in range(COLS)])
     *parts, column = tie(*parts, column)
     out = update(at_row, at_col, [inv, *parts], l11, l21, l22, column, column_other, strip, facing, view)

time: 87.2 us -> 83 us (0.952)
  the two profiles are of different devices: /device:TPU:57 before, /device:TPU:1 now
where the time goes in v3:
time: 83 us; the launch traced here: 82.3 us
  starting transfers between devices  36.8 us (44%)
  waiting for transfers between devices  20.6 us (25%)
  Pallas kernels  19.2 us (23%)
  local copies, waits for them, and re-layouts  3.76 us (5%)
  other arithmetic  1.31 us (2%)
    ppermute x13, starting transfers between devices, send(): return lax.ppermute(value, 'col', pairs)  22.2 us
    ppermute x5, starting transfers between devices, send_plane(): return lax.ppermute(value, ('row', 'col'), plane_pairs(first, second))  14.6 us
    pallas_call x1, Pallas kernels, factorise(): pl.pallas_call(factor_kernel, in_specs=[pl.BlockSpec(memory_space=pltpu.S...  11.9 us
    ppermute x13, waiting for transfers between devices, send(): return lax.ppermute(value, 'col', pairs)  11.5 us
    ppermute x5, waiting for transfers between devices, send_plane(): return lax.ppermute(value, ('row', 'col'), plane_pairs(first, second))  9.17 us
    pallas_call x1, Pallas kernels, update(): pl.pallas_call(update_kernel, in_specs=[smem] * 2 + [vmem] * 11 + [anywhe...  7.34 us
    slice x1, local copies, waits for them, and re-layouts, shards(): column = view.reshape(-1, 4, NB)[:, 0, :]  1.95 us
  transfers between devices with their start and end apart: 18, of which 9 were waited for; matrix products, arithmetic and copies ran while one was open for 4% of the time, Pallas kernels for 14%

profile of v3, /device:TPU:1, one launch (start us, length us, event | category | flops | bytes accessed | tf_op | source)
XLA Modules:
  0.0 82.3 jit_solution(1574945912384270245)
XLA Ops:
  0.0 1.0 %slice.12 = f32[1,1,128,1,4,128]{5,4,3,2,1,0:T(4,128)S(1)} slice(f32[1,8,128,1,4,128]{5,4,3,2,1,0:T(4,128)} %param.1), slice={[0:1], [0:1], [0:128], [0:1], [0:4], [0:128]} | slice | bytes 524288 | tf_op jit(solution)/shard_map/slice | solution.py:290
  1.0 5.7 %collective-permute-start = (f32[512,128]{1,0:T(8,128)S(1)}, f32[512,128]{1,0:T(8,128)S(1)}, u32[]{:S(2)}, u32[]{:S(2)}) collective-permute-start(f32[512,128]{1,0:T(8,128)S(1)} %bitcast.19), channel_id=1, source_target_pairs={{0,96},{32,64},{2,98},{34,66},{4,100},{36,68},{6,102},{38,70},{8,1... | collective-permute-start | bytes 786440 | tf_op jit(solution)/shard_map/ppermute | solution.py:282
  6.6 2.0 %slice.16 = f32[1024,1,128]{2,1,0:T(1,128)S(1)} slice(f32[1024,4,128]{2,1,0:T(4,128)} %bitcast.15), slice={[0:1024], [0:1], [0:128]} | slice | bytes 1048576 | tf_op jit(solution)/shard_map/slice | solution.py:292
  8.6 3.6 %collective-permute-start.5 = (f32[1024,128]{1,0:T(8,128)S(1)}, f32[1024,128]{1,0:T(8,128)S(1)}, u32[]{:S(2)}, u32[]{:S(2)}) collective-permute-start(f32[1024,128]{1,0:T(8,128)S(1)} %bitcast.17), channel_id=1, source_target_pairs={{0,2},{1,3},{32,34},{33,35},{64,66},{65,67},{96,98},{97,99},{128,1... | collective-permute-start | bytes 1572872 | tf_op jit(solution)/shard_map/ppermute | solution.py:279
  12.2 0.0 collective-permute-done
  12.3 1.3 %collective-permute-start.1 = (f32[512,128]{1,0:T(8,128)S(1)}, f32[512,128]{1,0:T(8,128)S(1)}, u32[]{:S(2)}, u32[]{:S(2)}) collective-permute-start(f32[512,128]{1,0:T(8,128)S(1)} %broadcast_select_fusion.3), channel_id=1, source_target_pairs={{0,256},{32,288},{64,320},{96,352},{2,258},{34,290},{66,322},{98,3... | collective-permute-start | bytes 786440 | tf_op jit(solution)/shard_map/ppermute | solution.py:282
  13.6 5.1 %collective-permute-done.1 = f32[512,128]{1,0:T(8,128)S(1)} collective-permute-done((f32[512,128]{1,0:T(8,128)S(1)}, f32[512,128]{1,0:T(8,128)S(1)}, u32[]{:S(2)}, u32[]{:S(2)}) %collective-permute-start.1) | collective-permute-done | bytes 262176 | tf_op jit(solution)/shard_map/ppermute | solution.py:282
  18.7 4.2 %collective-permute-done.5 = f32[1024,128]{1,0:T(8,128)S(1)} collective-permute-done((f32[1024,128]{1,0:T(8,128)S(1)}, f32[1024,128]{1,0:T(8,128)S(1)}, u32[]{:S(2)}, u32[]{:S(2)}) %collective-permute-start.5) | collective-permute-done | bytes 524320 | tf_op jit(solution)/shard_map/ppermute | solution.py:279
  22.9 0.7 collective-permute-start.6
  23.6 1.3 %collective-permute-start.2 = (f32[512,128]{1,0:T(8,128)S(1)}, f32[512,128]{1,0:T(8,128)S(1)}, u32[]{:S(2)}, u32[]{:S(2)}) collective-permute-start(f32[512,128]{1,0:T(8,128)S(1)} %broadcast_select_fusion.4), channel_id=1, source_target_pairs={{0,128},{32,160},{64,192},{96,224},{256,384},{288,416},{320,448},{... | collective-permute-start | bytes 786440 | tf_op jit(solution)/shard_map/ppermute | solution.py:282
  25.0 3.2 %collective-permute-done.2 = f32[512,128]{1,0:T(8,128)S(1)} collective-permute-done((f32[512,128]{1,0:T(8,128)S(1)}, f32[512,128]{1,0:T(8,128)S(1)}, u32[]{:S(2)}, u32[]{:S(2)}) %collective-permute-start.2) | collective-permute-done | bytes 262176 | tf_op jit(solution)/shard_map/ppermute | solution.py:282
  28.2 0.0 copy-start.1
  28.2 0.0 collective-permute-done.6
  28.2 0.1 broadcast_select_fusion
  28.3 0.7 collective-permute-start.7
  29.0 3.8 %collective-permute-start.3 = (f32[128,128]{1,0:T(8,128)S(1)}, f32[128,128]{1,0:T(8,128)S(1)}, u32[]{:S(2)}, u32[]{:S(2)}) collective-permute-start(f32[128,128]{1,0:T(8,128)S(1)} %slice.14), channel_id=1, source_target_pairs={{0,32},{32,0},{64,96},{96,64},{128,160},{160,128},{192,224},{224,1... | collective-permute-start | bytes 196616 | tf_op jit(solution)/shard_map/ppermute | solution.py:282
  32.9 0.0 collective-permute-done.7
  32.9 0.1 broadcast_select_fusion.1
  32.9 0.7 collective-permute-start.8
  33.7 0.9 %collective-permute-done.3 = f32[128,128]{1,0:T(8,128)S(1)} collective-permute-done((f32[128,128]{1,0:T(8,128)S(1)}, f32[128,128]{1,0:T(8,128)S(1)}, u32[]{:S(2)}, u32[]{:S(2)}) %collective-permute-start.3) | collective-permute-done | bytes 65568 | tf_op jit(solution)/shard_map/ppermute | solution.py:282
  34.5 0.0 copy-start.3
  34.5 4.6 %collective-permute-start.4 = (f32[2,128,128]{2,1,0:T(8,128)S(1)}, f32[2,128,128]{2,1,0:T(8,128)S(1)}, u32[]{:S(2)}, u32[]{:S(2)}) collective-permute-start(f32[2,128,128]{2,1,0:T(8,128)S(1)} %pad_maximum_fusion.own), channel_id=1, source_target_pairs={{0,1},{1,0},{32,33},{33,32},{64,65},{65,64},{96,97},{97,96},{128,1... | collective-permute-start | bytes 393224 | tf_op jit(solution)/shard_map/ppermute | solution.py:279
  39.1 2.5 %collective-permute-start.9 = (f32[512,128]{1,0:T(8,128)S(1)}, f32[512,128]{1,0:T(8,128)S(1)}, u32[]{:S(2)}, u32[]{:S(2)}) collective-permute-start(f32[512,128]{1,0:T(8,128)S(1)} %broadcast_select_fusion.5.here), channel_id=1, source_target_pairs={{0,32},{32,0},{64,96},{96,64},{128,160},{160,128},{192,224},{224,1... | collective-permute-start | bytes 786440 | tf_op jit(solution)/shard_map/ppermute | solution.py:282
  41.7 0.0 collective-permute-done.4.other
  41.7 0.0 copy-start.9
  41.7 0.0 collective-permute-done.8
  41.7 0.1 broadcast_select_fusion.2
  41.8 0.0 copy-done.1
  41.8 0.7 collective-permute-start.16
  42.5 0.0 copy-done.3
  42.5 0.0 copy-done.9
  42.5 11.9 %factorise.1 = (f32[264,128]{1,0:T(8,128)}, f32[128,128]{1,0:T(8,128)}, f32[128,128]{1,0:T(8,128)}, f32[128,128]{1,0:T(8,128)}) custom-call(s32[1]{0:T(128)} %bitcast.1.col.at_col, f32[2,128,128]{2,1,0:T(8,128)} %copy-done.3, f32[2,128,128]{2,1,0:T(8,128)} %copy-done.9), custom_call_target="tpu_custom_call" | custom-call | tf_op jit(solution)/shard_map/factorise/pallas_call | solution.py:140
  54.4 0.0 collective-permute-done.9.there
  54.4 0.0 copy-start.5
  54.4 1.3 %collective-permute-start.12 = (f32[264,128]{1,0:T(8,128)}, f32[264,128]{1,0:T(8,128)S(1)}, u32[]{:S(2)}, u32[]{:S(2)}) collective-permute-start(f32[264,128]{1,0:T(8,128)} %get-tuple-element.51), channel_id=1, source_target_pairs={{0,24},{1,9},{32,56},{33,41},{64,88},{65,73},{96,120},{97,105},{12... | collective-permute-start | bytes 405512 | tf_op jit(solution)/shard_map/ppermute | solution.py:279
  55.7 1.3 %collective-permute-start.11 = (f32[264,128]{1,0:T(8,128)}, f32[264,128]{1,0:T(8,128)S(1)}, u32[]{:S(2)}, u32[]{:S(2)}) collective-permute-start(f32[264,128]{1,0:T(8,128)} %get-tuple-element.51), channel_id=1, source_target_pairs={{0,8},{1,25},{32,40},{33,57},{64,72},{65,89},{96,104},{97,121},{12... | collective-permute-start | bytes 405512 | tf_op jit(solution)/shard_map/ppermute | solution.py:279
  57.0 1.3 %collective-permute-start.10 = (f32[264,128]{1,0:T(8,128)}, f32[264,128]{1,0:T(8,128)S(1)}, u32[]{:S(2)}, u32[]{:S(2)}) collective-permute-start(f32[264,128]{1,0:T(8,128)} %get-tuple-element.51), channel_id=1, source_target_pairs={{0,16},{1,17},{32,48},{33,49},{64,80},{65,81},{96,112},{97,113},{1... | collective-permute-start | bytes 405512 | tf_op jit(solution)/shard_map/ppermute | solution.py:279
  58.3 0.0 collective-permute-done.12
  58.3 1.5 %collective-permute-done.11 = f32[264,128]{1,0:T(8,128)S(1)} collective-permute-done((f32[264,128]{1,0:T(8,128)}, f32[264,128]{1,0:T(8,128)S(1)}, u32[]{:S(2)}, u32[]{:S(2)}) %collective-permute-start.11) | collective-permute-done | bytes 135200 | tf_op jit(solution)/shard_map/ppermute | solution.py:279
  59.9 2.1 %collective-permute-done.10 = f32[264,128]{1,0:T(8,128)S(1)} collective-permute-done((f32[264,128]{1,0:T(8,128)}, f32[264,128]{1,0:T(8,128)S(1)}, u32[]{:S(2)}, u32[]{:S(2)}) %collective-permute-start.10) | collective-permute-done | bytes 135200 | tf_op jit(solution)/shard_map/ppermute | solution.py:279
  61.9 1.0 %select_select_fusion.1.held = f32[264,128]{1,0:T(8,128)S(1)} fusion(f32[264,128]{1,0:T(8,128)S(1)} %collective-permute-done.11, f32[264,128]{1,0:T(8,128)S(1)} %collective-permute-done.12, f32[264,128]{1,0:T(8,128)S(1)} %collective-permute-done.10, f32[264,128]{1,0:T(8,128)} %get-tuple-element.51, pred[]{:T(512)S(6)} %eq.70, pred[]{:T(512)S(6)} %eq.69, ...), kind=kLoop, calls=%fused_computation.4 | loop fusion | flops 101376 | bytes 675843 | tf_op jit(solution)/shard_map/jit(_where)/select_n | solution.py:286
  62.9 0.0 copy-start.2
  62.9 2.3 %collective-permute-start.15 = (f32[264,128]{1,0:T(8,128)S(1)}, f32[264,128]{1,0:T(8,128)S(1)}, u32[]{:S(2)}, u32[]{:S(2)}) collective-permute-start(f32[264,128]{1,0:T(8,128)S(1)} %select_select_fusion.1.held), channel_id=1, source_target_pairs={{0,6},{1,27},{8,14},{25,19},{16,22},{17,11},{24,30},{9,3},{32,38},... | collective-permute-start | bytes 405512 | tf_op jit(solution)/shard_map/ppermute | solution.py:279
  65.2 1.3 %collective-permute-start.14 = (f32[264,128]{1,0:T(8,128)S(1)}, f32[264,128]{1,0:T(8,128)S(1)}, u32[]{:S(2)}, u32[]{:S(2)}) collective-permute-start(f32[264,128]{1,0:T(8,128)S(1)} %select_select_fusion.1.held), channel_id=1, source_target_pairs={{0,2},{1,31},{8,10},{25,23},{16,18},{17,15},{24,26},{9,7},{32,34},... | collective-permute-start | bytes 405512 | tf_op jit(solution)/shard_map/ppermute | solution.py:279
  66.5 1.3 %collective-permute-start.13 = (f32[264,128]{1,0:T(8,128)S(1)}, f32[264,128]{1,0:T(8,128)S(1)}, u32[]{:S(2)}, u32[]{:S(2)}) collective-permute-start(f32[264,128]{1,0:T(8,128)S(1)} %select_select_fusion.1.held), channel_id=1, source_target_pairs={{0,4},{1,29},{8,12},{25,21},{16,20},{17,13},{24,28},{9,5},{32,36},... | collective-permute-start | bytes 405512 | tf_op jit(solution)/shard_map/ppermute | solution.py:279
  67.8 0.0 collective-permute-done.16
  67.8 0.0 collective-permute-done.15.three
  67.8 0.0 copy-start.6
  67.8 0.7 collective-permute-done.14.one
  68.6 0.0 copy-start.7
  68.6 1.4 %collective-permute-done.13.two = f32[264,128]{1,0:T(8,128)S(1)} collective-permute-done((f32[264,128]{1,0:T(8,128)S(1)}, f32[264,128]{1,0:T(8,128)S(1)}, u32[]{:S(2)}, u32[]{:S(2)}) %collective-permute-start.13) | collective-permute-done | bytes 135200 | tf_op jit(solution)/shard_map/ppermute | solution.py:279
  70.0 0.0 copy-start.8
  70.0 0.1 select_select_fusion.own
  70.1 0.0 copy-start
  70.1 2.6 %collective-permute-start.17 = (f32[1024,128]{1,0:T(8,128)S(1)}, f32[1024,128]{1,0:T(8,128)S(1)}, u32[]{:S(2)}, u32[]{:S(2)}) collective-permute-start(f32[1024,128]{1,0:T(8,128)S(1)} %select_select_fusion.own), channel_id=1, source_target_pairs={{0,1},{1,0},{2,3},{3,2},{4,5},{5,4},{6,7},{7,6},{8,9},{9,8},{10,11... | collective-permute-start | bytes 1572872 | tf_op jit(solution)/shard_map/ppermute | solution.py:279
  72.7 1.5 %collective-permute-done.17.other = f32[1024,128]{1,0:T(8,128)S(1)} collective-permute-done((f32[1024,128]{1,0:T(8,128)S(1)}, f32[1024,128]{1,0:T(8,128)S(1)}, u32[]{:S(2)}, u32[]{:S(2)}) %collective-permute-start.17) | collective-permute-done | bytes 524320 | tf_op jit(solution)/shard_map/ppermute | solution.py:279
  74.2 0.0 copy-done.5
  74.2 0.0 copy-done.2
  74.2 0.0 copy-done.6
  74.2 0.0 copy-done.7
  74.2 0.0 copy-done.8
  74.2 0.0 copy-done
  74.2 0.8 copy-done.4
  75.0 7.3 %update.1 = f32[4096,128]{1,0:T(8,128)} custom-call(s32[1]{0:T(128)} %bitcast.at_row, s32[1]{0:T(128)} %bitcast.1.col.at_col, f32[264,128]{1,0:T(8,128)} %copy-done.2, f32[264,128]{1,0:T(8,128)} %copy-done.8, f32[264,128]{1,0:T(8,128)} %copy-done.7, f32[264,128]{1,0:T(8,128)} %copy-done.6, f32[128,128]{1,0:T(8,128)} %get-tuple-element.68.l11, ...), custom_call_target="tpu_custom_call" | custom-call | tf_op jit(solution)/shard_map/update/pallas_call | solution.py:232
  (7 shorter events, 0.1 us)
Async XLA Ops:
  1.0 11.3 %collective-permute-start = (f32[512,128]{1,0:T(8,128)S(1)}, f32[512,128]{1,0:T(8,128)S(1)}, u32[]{:S(2)}, u32[]{:S(2)}) collective-permute-start(f32[512,128]{1,0:T(8,128)S(1)} %bitcast.19), channel_id=1, source_target_pairs={{0,96},{32,64},{2,98},{34,66},{4,100},{36,68},{6,102},{38,70},{8,1... | collective-permute-start | bytes 786440 | tf_op jit(solution)/shard_map/ppermute | solution.py:282
  8.6 14.3 %collective-permute-start.5 = (f32[1024,128]{1,0:T(8,128)S(1)}, f32[1024,128]{1,0:T(8,128)S(1)}, u32[]{:S(2)}, u32[]{:S(2)}) collective-permute-start(f32[1024,128]{1,0:T(8,128)S(1)} %bitcast.17), channel_id=1, source_target_pairs={{0,2},{1,3},{32,34},{33,35},{64,66},{65,67},{96,98},{97,99},{128,1... | collective-permute-start | bytes 1572872 | tf_op jit(solution)/shard_map/ppermute | solution.py:279
  12.3 6.4 %collective-permute-start.1 = (f32[512,128]{1,0:T(8,128)S(1)}, f32[512,128]{1,0:T(8,128)S(1)}, u32[]{:S(2)}, u32[]{:S(2)}) collective-permute-start(f32[512,128]{1,0:T(8,128)S(1)} %broadcast_select_fusion.3), channel_id=1, source_target_pairs={{0,256},{32,288},{64,320},{96,352},{2,258},{34,290},{66,322},{98,3... | collective-permute-start | bytes 786440 | tf_op jit(solution)/shard_map/ppermute | solution.py:282
  22.9 5.3 %collective-permute-start.6 = (f32[1024,128]{1,0:T(8,128)S(1)}, f32[1024,128]{1,0:T(8,128)S(1)}, u32[]{:S(2)}, u32[]{:S(2)}) collective-permute-start(f32[1024,128]{1,0:T(8,128)S(1)} %collective-permute-done.5), channel_id=1, source_target_pairs={{2,10},{3,27},{34,42},{35,59},{66,74},{67,91},{98,106},{99,123},{1... | collective-permute-start | bytes 1572872 | tf_op jit(solution)/shard_map/ppermute | solution.py:279
  23.6 4.6 %collective-permute-start.2 = (f32[512,128]{1,0:T(8,128)S(1)}, f32[512,128]{1,0:T(8,128)S(1)}, u32[]{:S(2)}, u32[]{:S(2)}) collective-permute-start(f32[512,128]{1,0:T(8,128)S(1)} %broadcast_select_fusion.4), channel_id=1, source_target_pairs={{0,128},{32,160},{64,192},{96,224},{256,384},{288,416},{320,448},{... | collective-permute-start | bytes 786440 | tf_op jit(solution)/shard_map/ppermute | solution.py:282
  28.2 13.6 %copy-start.1 = (f32[512,128]{1,0:T(8,128)}, f32[512,128]{1,0:T(8,128)S(1)}, u32[]{:S(2)}) copy-start(f32[512,128]{1,0:T(8,128)S(1)} %broadcast_select_fusion.5.here) | copy-start | bytes 786436
  28.3 4.6 %collective-permute-start.7 = (f32[1024,128]{1,0:T(8,128)S(1)}, f32[1024,128]{1,0:T(8,128)S(1)}, u32[]{:S(2)}, u32[]{:S(2)}) collective-permute-start(f32[1024,128]{1,0:T(8,128)S(1)} %broadcast_select_fusion), channel_id=1, source_target_pairs={{2,26},{3,11},{10,18},{27,19},{34,58},{35,43},{42,50},{59,51},{66,... | collective-permute-start | bytes 1572872 | tf_op jit(solution)/shard_map/ppermute | solution.py:279
  29.0 5.5 %collective-permute-start.3 = (f32[128,128]{1,0:T(8,128)S(1)}, f32[128,128]{1,0:T(8,128)S(1)}, u32[]{:S(2)}, u32[]{:S(2)}) collective-permute-start(f32[128,128]{1,0:T(8,128)S(1)} %slice.14), channel_id=1, source_target_pairs={{0,32},{32,0},{64,96},{96,64},{128,160},{160,128},{192,224},{224,1... | collective-permute-start | bytes 196616 | tf_op jit(solution)/shard_map/ppermute | solution.py:282
  32.9 8.8 %collective-permute-start.8 = (f32[1024,128]{1,0:T(8,128)S(1)}, f32[1024,128]{1,0:T(8,128)S(1)}, u32[]{:S(2)}, u32[]{:S(2)}) collective-permute-start(f32[1024,128]{1,0:T(8,128)S(1)} %broadcast_select_fusion.1), channel_id=1, source_target_pairs={{2,6},{3,31},{10,14},{27,23},{18,22},{19,15},{26,30},{11,7},{34,38... | collective-permute-start | bytes 1572872 | tf_op jit(solution)/shard_map/ppermute | solution.py:279
  34.5 8.0 %copy-start.3 = (f32[2,128,128]{2,1,0:T(8,128)}, f32[2,128,128]{2,1,0:T(8,128)S(1)}, u32[]{:S(2)}) copy-start(f32[2,128,128]{2,1,0:T(8,128)S(1)} %pad_maximum_fusion.own) | copy-start | bytes 393220
  34.5 7.1 %collective-permute-start.4 = (f32[2,128,128]{2,1,0:T(8,128)S(1)}, f32[2,128,128]{2,1,0:T(8,128)S(1)}, u32[]{:S(2)}, u32[]{:S(2)}) collective-permute-start(f32[2,128,128]{2,1,0:T(8,128)S(1)} %pad_maximum_fusion.own), channel_id=1, source_target_pairs={{0,1},{1,0},{32,33},{33,32},{64,65},{65,64},{96,97},{97,96},{128,1... | collective-permute-start | bytes 393224 | tf_op jit(solution)/shard_map/ppermute | solution.py:279
  39.1 15.2 %collective-permute-start.9 = (f32[512,128]{1,0:T(8,128)S(1)}, f32[512,128]{1,0:T(8,128)S(1)}, u32[]{:S(2)}, u32[]{:S(2)}) collective-permute-start(f32[512,128]{1,0:T(8,128)S(1)} %broadcast_select_fusion.5.here), channel_id=1, source_target_pairs={{0,32},{32,0},{64,96},{96,64},{128,160},{160,128},{192,224},{224,1... | collective-permute-start | bytes 786440 | tf_op jit(solution)/shard_map/ppermute | solution.py:282
  41.7 0.8 copy-start.9
  41.8 26.0 %collective-permute-start.16 = (f32[1024,128]{1,0:T(8,128)S(1)}, f32[1024,128]{1,0:T(8,128)S(1)}, u32[]{:S(2)}, u32[]{:S(2)}) collective-permute-start(f32[1024,128]{1,0:T(8,128)S(1)} %broadcast_select_fusion.2), channel_id=1, source_target_pairs={{2,4},{6,8},{31,29},{10,12},{27,25},{14,16},{23,21},{18,20},{19,17... | collective-permute-start | bytes 1572872 | tf_op jit(solution)/shard_map/ppermute | solution.py:279
  54.4 19.8 %copy-start.5 = (f32[512,128]{1,0:T(8,128)}, f32[512,128]{1,0:T(8,128)S(1)}, u32[]{:S(2)}) copy-start(f32[512,128]{1,0:T(8,128)S(1)} %collective-permute-done.9.there) | copy-start | bytes 786436
  54.4 4.0 %collective-permute-start.12 = (f32[264,128]{1,0:T(8,128)}, f32[264,128]{1,0:T(8,128)S(1)}, u32[]{:S(2)}, u32[]{:S(2)}) collective-permute-start(f32[264,128]{1,0:T(8,128)} %get-tuple-element.51), channel_id=1, source_target_pairs={{0,24},{1,9},{32,56},{33,41},{64,88},{65,73},{96,120},{97,105},{12... | collective-permute-start | bytes 405512 | tf_op jit(solution)/shard_map/ppermute | solution.py:279
  55.7 4.2 %collective-permute-start.11 = (f32[264,128]{1,0:T(8,128)}, f32[264,128]{1,0:T(8,128)S(1)}, u32[]{:S(2)}, u32[]{:S(2)}) collective-permute-start(f32[264,128]{1,0:T(8,128)} %get-tuple-element.51), channel_id=1, source_target_pairs={{0,8},{1,25},{32,40},{33,57},{64,72},{65,89},{96,104},{97,121},{12... | collective-permute-start | bytes 405512 | tf_op jit(solution)/shard_map/ppermute | solution.py:279
  57.0 5.0 %collective-permute-start.10 = (f32[264,128]{1,0:T(8,128)}, f32[264,128]{1,0:T(8,128)S(1)}, u32[]{:S(2)}, u32[]{:S(2)}) collective-permute-start(f32[264,128]{1,0:T(8,128)} %get-tuple-element.51), channel_id=1, source_target_pairs={{0,16},{1,17},{32,48},{33,49},{64,80},{65,81},{96,112},{97,113},{1... | collective-permute-start | bytes 405512 | tf_op jit(solution)/shard_map/ppermute | solution.py:279
  62.9 11.3 %copy-start.2 = (f32[264,128]{1,0:T(8,128)}, f32[264,128]{1,0:T(8,128)S(1)}, u32[]{:S(2)}) copy-start(f32[264,128]{1,0:T(8,128)S(1)} %select_select_fusion.1.held) | copy-start | bytes 405508
  62.9 4.9 %collective-permute-start.15 = (f32[264,128]{1,0:T(8,128)S(1)}, f32[264,128]{1,0:T(8,128)S(1)}, u32[]{:S(2)}, u32[]{:S(2)}) collective-permute-start(f32[264,128]{1,0:T(8,128)S(1)} %select_select_fusion.1.held), channel_id=1, source_target_pairs={{0,6},{1,27},{8,14},{25,19},{16,22},{17,11},{24,30},{9,3},{32,38},... | collective-permute-start | bytes 405512 | tf_op jit(solution)/shard_map/ppermute | solution.py:279
  65.2 3.4 %collective-permute-start.14 = (f32[264,128]{1,0:T(8,128)S(1)}, f32[264,128]{1,0:T(8,128)S(1)}, u32[]{:S(2)}, u32[]{:S(2)}) collective-permute-start(f32[264,128]{1,0:T(8,128)S(1)} %select_select_fusion.1.held), channel_id=1, source_target_pairs={{0,2},{1,31},{8,10},{25,23},{16,18},{17,15},{24,26},{9,7},{32,34},... | collective-permute-start | bytes 405512 | tf_op jit(solution)/shard_map/ppermute | solution.py:279
  66.5 3.5 %collective-permute-start.13 = (f32[264,128]{1,0:T(8,128)S(1)}, f32[264,128]{1,0:T(8,128)S(1)}, u32[]{:S(2)}, u32[]{:S(2)}) collective-permute-start(f32[264,128]{1,0:T(8,128)S(1)} %select_select_fusion.1.held), channel_id=1, source_target_pairs={{0,4},{1,29},{8,12},{25,21},{16,20},{17,13},{24,28},{9,5},{32,36},... | collective-permute-start | bytes 405512 | tf_op jit(solution)/shard_map/ppermute | solution.py:279
  67.8 6.4 %copy-start.6 = (f32[264,128]{1,0:T(8,128)}, f32[264,128]{1,0:T(8,128)S(1)}, u32[]{:S(2)}) copy-start(f32[264,128]{1,0:T(8,128)S(1)} %collective-permute-done.15.three) | copy-start | bytes 405508
  68.6 5.6 %copy-start.7 = (f32[264,128]{1,0:T(8,128)}, f32[264,128]{1,0:T(8,128)S(1)}, u32[]{:S(2)}) copy-start(f32[264,128]{1,0:T(8,128)S(1)} %collective-permute-done.14.one) | copy-start | bytes 405508
  70.0 4.2 %copy-start.8 = (f32[264,128]{1,0:T(8,128)}, f32[264,128]{1,0:T(8,128)S(1)}, u32[]{:S(2)}) copy-start(f32[264,128]{1,0:T(8,128)S(1)} %collective-permute-done.13.two) | copy-start | bytes 405508
  70.1 4.1 %copy-start = (f32[1024,128]{1,0:T(8,128)}, f32[1024,128]{1,0:T(8,128)S(1)}, u32[]{:S(2)}) copy-start(f32[1024,128]{1,0:T(8,128)S(1)} %select_select_fusion.own) | copy-start | bytes 1572868
  70.1 4.1 %collective-permute-start.17 = (f32[1024,128]{1,0:T(8,128)S(1)}, f32[1024,128]{1,0:T(8,128)S(1)}, u32[]{:S(2)}, u32[]{:S(2)}) collective-permute-start(f32[1024,128]{1,0:T(8,128)S(1)} %select_select_fusion.own), channel_id=1, source_target_pairs={{0,1},{1,0},{2,3},{3,2},{4,5},{5,4},{6,7},{7,6},{8,9},{9,8},{10,11... | collective-permute-start | bytes 1572872 | tf_op jit(solution)/shard_map/ppermute | solution.py:279
  74.2 0.8 copy-start.4

commit v4 on v3

--- a/solution.py
+++ b/solution.py
@@ -101,29 +101,37 @@
     return i11, -mm(i22, t21), i22
 
 
-def factor_kernel(col, own, other, packed, l11, l21, l22, work, upper, inv):
+def factor_kernel(col, own, other, packed, l11, l21, l22, work, upper, inv, blocks, sems):
     h, n = HALF, NB
     even = col[0] == 0
 
-    def block(side, half):
-        a, b = own[half], other[half]
-        return jnp.where(even, a, b) if side == 0 else jnp.where(even, b, a)
-
-    def put(to, blocks):
-        to[:h, :h] = blocks[0]
+    def put(to, parts):
+        to[:h, :h] = parts[0]
         to[:h, h:] = jnp.zeros((h, h), jnp.float32)
-        to[h:, :h] = blocks[1]
-        to[h:, h:] = blocks[2]
+        to[h:, :h] = parts[1]
+        to[h:, h:] = parts[2]
 
     @pl.when(col[0] < 2)
     def _():
-        put(inv.at[0], factor_block(block(0, 0), work, upper))
+        for i, (first, second, half) in enumerate(((own, other, 0), (own, other, 1), (other, own, 1))):
+
+            @pl.when(even)
+            def _():
+                pltpu.make_async_copy(first.at[half], blocks.at[i], sems.at[i]).start()
+
+            @pl.when(jnp.logical_not(even))
+            def _():
+                pltpu.make_async_copy(second.at[half], blocks.at[i], sems.at[i]).start()
+
+        for i in range(3):
+            pltpu.make_async_copy(own.at[0], blocks.at[i], sems.at[i]).wait()
+        put(inv.at[0], factor_block(blocks[0], work, upper))
         l11[...] = upper[...].T
         i11 = inv[0]
-        p = mmt(block(0, 1), i11)
+        p = mmt(blocks[1], i11)
         t = mm(p, i11)
         l21[...] = p
-        put(inv.at[1], factor_block(block(1, 1) - mmt(p, p), work, upper))
+        put(inv.at[1], factor_block(blocks[2] - mmt(p, p), work, upper))
         l22[...] = upper[...].T
         i22 = inv[1]
         r = lax.broadcasted_iota(jnp.int32, (n, n), 0)
@@ -139,13 +147,15 @@
     vmem = pl.BlockSpec(memory_space=pltpu.VMEM)
     return pl.pallas_call(
         factor_kernel,
-        in_specs=[pl.BlockSpec(memory_space=pltpu.SMEM), vmem, vmem],
+        in_specs=[pl.BlockSpec(memory_space=pltpu.SMEM)] + [pl.BlockSpec(memory_space=pl.ANY)] * 2,
         out_specs=[vmem] * 4,
         out_shape=[jax.ShapeDtypeStruct((2 * NB + 8, NB), jnp.float32), block, block, block],
         scratch_shapes=[
             pltpu.VMEM((HALF, NB), jnp.float32),
             pltpu.VMEM((NB, NB), jnp.float32),
             pltpu.VMEM((2, NB, NB), jnp.float32),
+            pltpu.VMEM((3, NB, NB), jnp.float32),
+            pltpu.SemaphoreType.DMA((3,)),
         ],
         name="factorise",
     )(col, own, other)
@@ -156,30 +166,48 @@
     return (x == 0) | (x == SIDE - 1)
 
 
-def update_kernel(at_row, at_col, held, two, one, three, l11, l21, l22, own, other, here, there, store, out, data, sems, outs):
+def update_kernel(at_row, at_col, held, two, one, three, l11, l21, l22, own, other, here, there, store, out, *scratch):
+    data, columns, strips, packed, corners, loads, saves, sems = scratch
     n = NB
-    chunks = data.shape[0]
-    rows_of = data.shape[1]
-    loads = [pltpu.make_async_copy(store.at[pl.ds(i * rows_of, rows_of)], data.at[i], sems.at[i]) for i in range(chunks)]
-    saves = [pltpu.make_async_copy(data.at[i], out.at[pl.ds(i * rows_of, rows_of)], outs.at[i]) for i in range(chunks)]
-    for load in loads:
-        load.start()
+    chunks, rows_of = data.shape[:2]
     row, col = at_row[0], at_col[0]
-    even = col % 2 == 0
-    top = is_top(row)
-    halves = [[], []]
-    for j in range(4):
-        a = here[pl.ds(j, n, stride=4), :]
-        b = there[pl.ds(j, n, stride=4), :]
-        halves[0].append(jnp.where(top, a, b))
-        halves[1].append(jnp.where(top, b, a))
-    whole = jnp.concatenate([jnp.concatenate(h, axis=1) for h in halves], axis=0)
+    core, z = col % 2, col // 2
+    step = jnp.where(core == 0, z, LAYERS - z) % 4
+    even, top = core == 0, is_top(row)
+
+    def start(condition, source, target, sem):
+        @pl.when(condition)
+        def _():
+            pltpu.make_async_copy(source, target, sem).start()
+
+    for i, part in enumerate((held, one, two, three)):
+        start(step == i, part, packed, sems.at[0])
+    for i, (near, far) in enumerate(((here, there), (there, here))):
+        start(top, near, strips.at[i], sems.at[1 + i])
+        start(jnp.logical_not(top), far, strips.at[i], sems.at[1 + i])
+    for i, (near, far) in enumerate(((own, other), (other, own))):
+        start(even, near, columns.at[i], sems.at[3 + i])
+        start(jnp.logical_not(even), far, columns.at[i], sems.at[3 + i])
+    fetch = [
+        pltpu.make_async_copy(store.at[pl.ds(i * rows_of, rows_of)], data.at[i], loads.at[i])
+        for i in range(chunks)
+    ]
+    save = [
+        pltpu.make_async_copy(data.at[i], out.at[pl.ds(i * rows_of, rows_of)], saves.at[i])
+        for i in range(chunks)
+    ]
+    for copy in fetch:
+        copy.start()
+    final = [pltpu.make_async_copy(l, corners.at[i], sems.at[5 + i]) for i, l in enumerate((l11, l21, l22))]
+
+    @pl.when(col < 2)
+    def _():
+        for copy in final:
+            copy.start()
+
+    pltpu.make_async_copy(held, packed, sems.at[0]).wait()
     r = lax.broadcasted_iota(jnp.int32, (n, n), 0)
     c = lax.broadcasted_iota(jnp.int32, (n, n), 1)
-    core, z = col % 2, col // 2
-    step = jnp.where(core == 0, z, LAYERS - z) % 4
-    packed = jnp.where(step == 2, two[...], held[...])
-    packed = jnp.where(step == 1, one[...], jnp.where(step == 3, three[...], packed))
     shared = packed[:n]
     i11 = jnp.where(r >= c, shared, 0.0)
     diagonal = jnp.where(r == c, packed[2 * n : 2 * n + 1], 0.0)
@@ -191,19 +219,23 @@
         ],
         axis=0,
     )
-    mirrored = split(mm(inverse, whole))
+    halves = []
+    for i in range(2):
+        pltpu.make_async_copy(here, strips.at[i], sems.at[1 + i]).wait()
+        halves.append(jnp.concatenate([strips[i, pl.ds(j, n, stride=4), :] for j in range(4)], axis=1))
+    mirrored = split(mm(inverse, jnp.concatenate(halves, axis=0)))
+    for i in range(2):
+        pltpu.make_async_copy(own, columns.at[i], sems.at[3 + i]).wait()
     count = rows_of // 4
     local = lax.broadcasted_iota(jnp.int32, (count, n), 0)
     lane = lax.broadcasted_iota(jnp.int32, (count, n), 1)
     for i in range(chunks):
         span = pl.ds(i * count, count)
-        a, b = own[span, :], other[span, :]
-        left, right = jnp.where(even, a, b), jnp.where(even, b, a)
-        panel = mmt(jnp.concatenate([left, right], axis=1), inverse)
+        panel = mmt(jnp.concatenate([columns[0, span, :], columns[1, span, :]], axis=1), inverse)
         update = mm3(panel, mirrored)
         grow = (i * (count // n) + local // n) * ROWS + row
         rid = grow * n + local % n
-        loads[i].wait()
+        fetch[i].wait()
         for j in range(4):
             cid = (j * COLS + col) * n + lane
             rows = pl.ds(j, count, stride=4)
@@ -214,30 +246,36 @@
         def _():
             solved = jnp.where(col == 0, panel[:, :n], panel[:, n:])
             if i == 0:
-                first = jnp.where(col == 0, l11[...], 0.0)
-                second = jnp.where(col == 0, l21[...], l22[...])
+                for copy in final:
+                    copy.wait()
+                first = jnp.where(col == 0, corners[0], 0.0)
+                second = jnp.where(col == 0, corners[1], corners[2])
                 solved = jnp.where(grow == 0, jnp.tile(first, (count // n, 1)), solved)
                 solved = jnp.where(grow == 1, jnp.tile(second, (count // n, 1)), solved)
             data[i, pl.ds(0, count, stride=4), :] = jnp.where(rid >= col * n + lane, solved, 0.0)
 
-        saves[i].start()
-    for save in saves:
-        save.wait()
+        save[i].start()
+    for copy in save:
+        copy.wait()
 
 
 def update(row, col, inverse, l11, l21, l22, own, other, here, there, view):
-    vmem = pl.BlockSpec(memory_space=pltpu.VMEM)
     smem = pl.BlockSpec(memory_space=pltpu.SMEM)
     anywhere = pl.BlockSpec(memory_space=pl.ANY)
     return pl.pallas_call(
         update_kernel,
-        in_specs=[smem] * 2 + [vmem] * 11 + [anywhere],
+        in_specs=[smem] * 2 + [anywhere] * 12,
         out_specs=anywhere,
         out_shape=jax.ShapeDtypeStruct(view.shape, jnp.float32),
         scratch_shapes=[
             pltpu.VMEM((CHUNKS, view.shape[0] // CHUNKS, NB), jnp.float32),
+            pltpu.VMEM((2, *own.shape), jnp.float32),
+            pltpu.VMEM((2, *here.shape), jnp.float32),
+            pltpu.VMEM(inverse[0].shape, jnp.float32),
+            pltpu.VMEM((3, NB, NB), jnp.float32),
             pltpu.SemaphoreType.DMA((CHUNKS,)),
             pltpu.SemaphoreType.DMA((CHUNKS,)),
+            pltpu.SemaphoreType.DMA((8,)),
         ],
         name="update",
     )(row, col, *inverse, l11, l21, l22, own, other, here, there, view)

time: 83 us -> 82.6 us (level)
  no operation moved by 1% of the time
where the time goes in v4:
time: 82.6 us; the launch traced here: 81.9 us
  starting transfers between devices  36.8 us (45%)
  waiting for transfers between devices  20.6 us (25%)
  Pallas kernels  18.8 us (23%)
  local copies, waits for them, and re-layouts  3.76 us (5%)
  other arithmetic  1.31 us (2%)
    ppermute x13, starting transfers between devices, send(): return lax.ppermute(value, 'col', pairs)  22.2 us
    ppermute x5, starting transfers between devices, send_plane(): return lax.ppermute(value, ('row', 'col'), plane_pairs(first, second))  14.6 us
    pallas_call x1, Pallas kernels, factorise(): pl.pallas_call(factor_kernel, in_specs=[pl.BlockSpec(memory_space=pltpu.S...  11.8 us
    ppermute x13, waiting for transfers between devices, send(): return lax.ppermute(value, 'col', pairs)  11.5 us
    ppermute x5, waiting for transfers between devices, send_plane(): return lax.ppermute(value, ('row', 'col'), plane_pairs(first, second))  9.17 us
    pallas_call x1, Pallas kernels, update(): pl.pallas_call(update_kernel, in_specs=[smem] * 2 + [anywhere] * 12, out_...  6.93 us
    slice x1, local copies, waits for them, and re-layouts, shards(): column = view.reshape(-1, 4, NB)[:, 0, :]  1.95 us
  transfers between devices with their start and end apart: 18, of which 9 were waited for; matrix products, arithmetic and copies ran while one was open for 4% of the time, Pallas kernels for 14%

profile of v4, /device:TPU:1, one launch (start us, length us, event | category | flops | bytes accessed | tf_op | source)
XLA Modules:
  0.0 81.9 jit_solution(11397307048244538605)
XLA Ops:
  0.0 1.0 %slice.12 = f32[1,1,128,1,4,128]{5,4,3,2,1,0:T(4,128)S(1)} slice(f32[1,8,128,1,4,128]{5,4,3,2,1,0:T(4,128)} %param.1), slice={[0:1], [0:1], [0:128], [0:1], [0:4], [0:128]} | slice | bytes 524288 | tf_op jit(solution)/shard_map/slice | solution.py:328
  1.0 5.7 %collective-permute-start = (f32[512,128]{1,0:T(8,128)S(1)}, f32[512,128]{1,0:T(8,128)S(1)}, u32[]{:S(2)}, u32[]{:S(2)}) collective-permute-start(f32[512,128]{1,0:T(8,128)S(1)} %bitcast.19), channel_id=1, source_target_pairs={{0,96},{32,64},{2,98},{34,66},{4,100},{36,68},{6,102},{38,70},{8,1... | collective-permute-start | bytes 786440 | tf_op jit(solution)/shard_map/ppermute | solution.py:320
  6.6 2.0 %slice.16 = f32[1024,1,128]{2,1,0:T(1,128)S(1)} slice(f32[1024,4,128]{2,1,0:T(4,128)} %bitcast.15), slice={[0:1024], [0:1], [0:128]} | slice | bytes 1048576 | tf_op jit(solution)/shard_map/slice | solution.py:330
  8.6 3.6 %collective-permute-start.5 = (f32[1024,128]{1,0:T(8,128)S(1)}, f32[1024,128]{1,0:T(8,128)S(1)}, u32[]{:S(2)}, u32[]{:S(2)}) collective-permute-start(f32[1024,128]{1,0:T(8,128)S(1)} %bitcast.17), channel_id=1, source_target_pairs={{0,2},{1,3},{32,34},{33,35},{64,66},{65,67},{96,98},{97,99},{128,1... | collective-permute-start | bytes 1572872 | tf_op jit(solution)/shard_map/ppermute | solution.py:317
  12.2 0.0 collective-permute-done
  12.3 1.3 %collective-permute-start.1 = (f32[512,128]{1,0:T(8,128)S(1)}, f32[512,128]{1,0:T(8,128)S(1)}, u32[]{:S(2)}, u32[]{:S(2)}) collective-permute-start(f32[512,128]{1,0:T(8,128)S(1)} %broadcast_select_fusion.3), channel_id=1, source_target_pairs={{0,256},{32,288},{64,320},{96,352},{2,258},{34,290},{66,322},{98,3... | collective-permute-start | bytes 786440 | tf_op jit(solution)/shard_map/ppermute | solution.py:320
  13.6 5.1 %collective-permute-done.1 = f32[512,128]{1,0:T(8,128)S(1)} collective-permute-done((f32[512,128]{1,0:T(8,128)S(1)}, f32[512,128]{1,0:T(8,128)S(1)}, u32[]{:S(2)}, u32[]{:S(2)}) %collective-permute-start.1) | collective-permute-done | bytes 262176 | tf_op jit(solution)/shard_map/ppermute | solution.py:320
  18.7 4.2 %collective-permute-done.5 = f32[1024,128]{1,0:T(8,128)S(1)} collective-permute-done((f32[1024,128]{1,0:T(8,128)S(1)}, f32[1024,128]{1,0:T(8,128)S(1)}, u32[]{:S(2)}, u32[]{:S(2)}) %collective-permute-start.5) | collective-permute-done | bytes 524320 | tf_op jit(solution)/shard_map/ppermute | solution.py:317
  22.9 0.7 collective-permute-start.6
  23.6 1.3 %collective-permute-start.2 = (f32[512,128]{1,0:T(8,128)S(1)}, f32[512,128]{1,0:T(8,128)S(1)}, u32[]{:S(2)}, u32[]{:S(2)}) collective-permute-start(f32[512,128]{1,0:T(8,128)S(1)} %broadcast_select_fusion.4), channel_id=1, source_target_pairs={{0,128},{32,160},{64,192},{96,224},{256,384},{288,416},{320,448},{... | collective-permute-start | bytes 786440 | tf_op jit(solution)/shard_map/ppermute | solution.py:320
  25.0 3.2 %collective-permute-done.2 = f32[512,128]{1,0:T(8,128)S(1)} collective-permute-done((f32[512,128]{1,0:T(8,128)S(1)}, f32[512,128]{1,0:T(8,128)S(1)}, u32[]{:S(2)}, u32[]{:S(2)}) %collective-permute-start.2) | collective-permute-done | bytes 262176 | tf_op jit(solution)/shard_map/ppermute | solution.py:320
  28.2 0.0 copy-start.1
  28.2 0.0 collective-permute-done.6
  28.2 0.1 broadcast_select_fusion
  28.3 0.7 collective-permute-start.7
  29.0 3.8 %collective-permute-start.3 = (f32[128,128]{1,0:T(8,128)S(1)}, f32[128,128]{1,0:T(8,128)S(1)}, u32[]{:S(2)}, u32[]{:S(2)}) collective-permute-start(f32[128,128]{1,0:T(8,128)S(1)} %slice.14), channel_id=1, source_target_pairs={{0,32},{32,0},{64,96},{96,64},{128,160},{160,128},{192,224},{224,1... | collective-permute-start | bytes 196616 | tf_op jit(solution)/shard_map/ppermute | solution.py:320
  32.9 0.0 collective-permute-done.7
  32.9 0.1 broadcast_select_fusion.1
  32.9 0.7 collective-permute-start.8
  33.7 0.9 %collective-permute-done.3 = f32[128,128]{1,0:T(8,128)S(1)} collective-permute-done((f32[128,128]{1,0:T(8,128)S(1)}, f32[128,128]{1,0:T(8,128)S(1)}, u32[]{:S(2)}, u32[]{:S(2)}) %collective-permute-start.3) | collective-permute-done | bytes 65568 | tf_op jit(solution)/shard_map/ppermute | solution.py:320
  34.5 0.0 copy-start.3
  34.5 4.6 %collective-permute-start.4 = (f32[2,128,128]{2,1,0:T(8,128)S(1)}, f32[2,128,128]{2,1,0:T(8,128)S(1)}, u32[]{:S(2)}, u32[]{:S(2)}) collective-permute-start(f32[2,128,128]{2,1,0:T(8,128)S(1)} %pad_maximum_fusion.own), channel_id=1, source_target_pairs={{0,1},{1,0},{32,33},{33,32},{64,65},{65,64},{96,97},{97,96},{128,1... | collective-permute-start | bytes 393224 | tf_op jit(solution)/shard_map/ppermute | solution.py:317
  39.1 2.5 %collective-permute-start.9 = (f32[512,128]{1,0:T(8,128)S(1)}, f32[512,128]{1,0:T(8,128)S(1)}, u32[]{:S(2)}, u32[]{:S(2)}) collective-permute-start(f32[512,128]{1,0:T(8,128)S(1)} %broadcast_select_fusion.5.here), channel_id=1, source_target_pairs={{0,32},{32,0},{64,96},{96,64},{128,160},{160,128},{192,224},{224,1... | collective-permute-start | bytes 786440 | tf_op jit(solution)/shard_map/ppermute | solution.py:320
  41.7 0.0 collective-permute-done.4.other
  41.7 0.0 copy-start.9
  41.7 0.0 collective-permute-done.8
  41.7 0.1 broadcast_select_fusion.2
  41.8 0.0 copy-done.1
  41.8 0.7 collective-permute-start.16
  42.5 0.0 copy-done.3
  42.5 0.0 copy-done.9
  42.5 11.8 %factorise.1 = (f32[264,128]{1,0:T(8,128)}, f32[128,128]{1,0:T(8,128)}, f32[128,128]{1,0:T(8,128)}, f32[128,128]{1,0:T(8,128)}) custom-call(s32[1]{0:T(128)} %bitcast.1.col.at_col, f32[2,128,128]{2,1,0:T(8,128)} %copy-done.3, f32[2,128,128]{2,1,0:T(8,128)} %copy-done.9), custom_call_target="tpu_custom_call" | custom-call | tf_op jit(solution)/shard_map/factorise/pallas_call | solution.py:148
  54.3 0.0 collective-permute-done.9.there
  54.4 0.0 copy-start.5
  54.4 1.3 %collective-permute-start.12 = (f32[264,128]{1,0:T(8,128)}, f32[264,128]{1,0:T(8,128)S(1)}, u32[]{:S(2)}, u32[]{:S(2)}) collective-permute-start(f32[264,128]{1,0:T(8,128)} %get-tuple-element.51), channel_id=1, source_target_pairs={{0,24},{1,9},{32,56},{33,41},{64,88},{65,73},{96,120},{97,105},{12... | collective-permute-start | bytes 405512 | tf_op jit(solution)/shard_map/ppermute | solution.py:317
  55.7 1.3 %collective-permute-start.11 = (f32[264,128]{1,0:T(8,128)}, f32[264,128]{1,0:T(8,128)S(1)}, u32[]{:S(2)}, u32[]{:S(2)}) collective-permute-start(f32[264,128]{1,0:T(8,128)} %get-tuple-element.51), channel_id=1, source_target_pairs={{0,8},{1,25},{32,40},{33,57},{64,72},{65,89},{96,104},{97,121},{12... | collective-permute-start | bytes 405512 | tf_op jit(solution)/shard_map/ppermute | solution.py:317
  57.0 1.3 %collective-permute-start.10 = (f32[264,128]{1,0:T(8,128)}, f32[264,128]{1,0:T(8,128)S(1)}, u32[]{:S(2)}, u32[]{:S(2)}) collective-permute-start(f32[264,128]{1,0:T(8,128)} %get-tuple-element.51), channel_id=1, source_target_pairs={{0,16},{1,17},{32,48},{33,49},{64,80},{65,81},{96,112},{97,113},{1... | collective-permute-start | bytes 405512 | tf_op jit(solution)/shard_map/ppermute | solution.py:317
  58.3 0.0 collective-permute-done.12
  58.3 1.5 %collective-permute-done.11 = f32[264,128]{1,0:T(8,128)S(1)} collective-permute-done((f32[264,128]{1,0:T(8,128)}, f32[264,128]{1,0:T(8,128)S(1)}, u32[]{:S(2)}, u32[]{:S(2)}) %collective-permute-start.11) | collective-permute-done | bytes 135200 | tf_op jit(solution)/shard_map/ppermute | solution.py:317
  59.9 2.1 %collective-permute-done.10 = f32[264,128]{1,0:T(8,128)S(1)} collective-permute-done((f32[264,128]{1,0:T(8,128)}, f32[264,128]{1,0:T(8,128)S(1)}, u32[]{:S(2)}, u32[]{:S(2)}) %collective-permute-start.10) | collective-permute-done | bytes 135200 | tf_op jit(solution)/shard_map/ppermute | solution.py:317
  61.9 1.0 %select_select_fusion.1.held = f32[264,128]{1,0:T(8,128)S(1)} fusion(f32[264,128]{1,0:T(8,128)S(1)} %collective-permute-done.11, f32[264,128]{1,0:T(8,128)S(1)} %collective-permute-done.12, f32[264,128]{1,0:T(8,128)S(1)} %collective-permute-done.10, f32[264,128]{1,0:T(8,128)} %get-tuple-element.51, pred[]{:T(512)S(6)} %eq.70, pred[]{:T(512)S(6)} %eq.69, ...), kind=kLoop, calls=%fused_computation.4 | loop fusion | flops 101376 | bytes 675843 | tf_op jit(solution)/shard_map/jit(_where)/select_n | solution.py:324
  62.9 0.0 copy-start.2
  62.9 2.3 %collective-permute-start.15 = (f32[264,128]{1,0:T(8,128)S(1)}, f32[264,128]{1,0:T(8,128)S(1)}, u32[]{:S(2)}, u32[]{:S(2)}) collective-permute-start(f32[264,128]{1,0:T(8,128)S(1)} %select_select_fusion.1.held), channel_id=1, source_target_pairs={{0,6},{1,27},{8,14},{25,19},{16,22},{17,11},{24,30},{9,3},{32,38},... | collective-permute-start | bytes 405512 | tf_op jit(solution)/shard_map/ppermute | solution.py:317
  65.2 1.3 %collective-permute-start.14 = (f32[264,128]{1,0:T(8,128)S(1)}, f32[264,128]{1,0:T(8,128)S(1)}, u32[]{:S(2)}, u32[]{:S(2)}) collective-permute-start(f32[264,128]{1,0:T(8,128)S(1)} %select_select_fusion.1.held), channel_id=1, source_target_pairs={{0,2},{1,31},{8,10},{25,23},{16,18},{17,15},{24,26},{9,7},{32,34},... | collective-permute-start | bytes 405512 | tf_op jit(solution)/shard_map/ppermute | solution.py:317
  66.5 1.3 %collective-permute-start.13 = (f32[264,128]{1,0:T(8,128)S(1)}, f32[264,128]{1,0:T(8,128)S(1)}, u32[]{:S(2)}, u32[]{:S(2)}) collective-permute-start(f32[264,128]{1,0:T(8,128)S(1)} %select_select_fusion.1.held), channel_id=1, source_target_pairs={{0,4},{1,29},{8,12},{25,21},{16,20},{17,13},{24,28},{9,5},{32,36},... | collective-permute-start | bytes 405512 | tf_op jit(solution)/shard_map/ppermute | solution.py:317
  67.8 0.0 collective-permute-done.16
  67.8 0.0 collective-permute-done.15.three
  67.8 0.0 copy-start.6
  67.8 0.7 collective-permute-done.14.one
  68.6 0.0 copy-start.7
  68.6 1.4 %collective-permute-done.13.two = f32[264,128]{1,0:T(8,128)S(1)} collective-permute-done((f32[264,128]{1,0:T(8,128)S(1)}, f32[264,128]{1,0:T(8,128)S(1)}, u32[]{:S(2)}, u32[]{:S(2)}) %collective-permute-start.13) | collective-permute-done | bytes 135200 | tf_op jit(solution)/shard_map/ppermute | solution.py:317
  70.0 0.0 copy-start.8
  70.0 0.1 select_select_fusion.own
  70.1 0.0 copy-start
  70.1 2.6 %collective-permute-start.17 = (f32[1024,128]{1,0:T(8,128)S(1)}, f32[1024,128]{1,0:T(8,128)S(1)}, u32[]{:S(2)}, u32[]{:S(2)}) collective-permute-start(f32[1024,128]{1,0:T(8,128)S(1)} %select_select_fusion.own), channel_id=1, source_target_pairs={{0,1},{1,0},{2,3},{3,2},{4,5},{5,4},{6,7},{7,6},{8,9},{9,8},{10,11... | collective-permute-start | bytes 1572872 | tf_op jit(solution)/shard_map/ppermute | solution.py:317
  72.6 1.5 %collective-permute-done.17.other = f32[1024,128]{1,0:T(8,128)S(1)} collective-permute-done((f32[1024,128]{1,0:T(8,128)S(1)}, f32[1024,128]{1,0:T(8,128)S(1)}, u32[]{:S(2)}, u32[]{:S(2)}) %collective-permute-start.17) | collective-permute-done | bytes 524320 | tf_op jit(solution)/shard_map/ppermute | solution.py:317
  74.2 0.0 copy-done.5
  74.2 0.0 copy-done.2
  74.2 0.0 copy-done.6
  74.2 0.0 copy-done.7
  74.2 0.0 copy-done.8
  74.2 0.0 copy-done
  74.2 0.8 copy-done.4
  75.0 6.9 %update.1 = f32[4096,128]{1,0:T(8,128)} custom-call(s32[1]{0:T(128)} %bitcast.at_row, s32[1]{0:T(128)} %bitcast.1.col.at_col, f32[264,128]{1,0:T(8,128)} %copy-done.2, f32[264,128]{1,0:T(8,128)} %copy-done.8, f32[264,128]{1,0:T(8,128)} %copy-done.7, f32[264,128]{1,0:T(8,128)} %copy-done.6, f32[128,128]{1,0:T(8,128)} %get-tuple-element.68.l11, ...), custom_call_target="tpu_custom_call" | custom-call | tf_op jit(solution)/shard_map/update/pallas_call | solution.py:265
  (7 shorter events, 0.1 us)
Async XLA Ops:
  1.0 11.3 %collective-permute-start = (f32[512,128]{1,0:T(8,128)S(1)}, f32[512,128]{1,0:T(8,128)S(1)}, u32[]{:S(2)}, u32[]{:S(2)}) collective-permute-start(f32[512,128]{1,0:T(8,128)S(1)} %bitcast.19), channel_id=1, source_target_pairs={{0,96},{32,64},{2,98},{34,66},{4,100},{36,68},{6,102},{38,70},{8,1... | collective-permute-start | bytes 786440 | tf_op jit(solution)/shard_map/ppermute | solution.py:320
  8.6 14.3 %collective-permute-start.5 = (f32[1024,128]{1,0:T(8,128)S(1)}, f32[1024,128]{1,0:T(8,128)S(1)}, u32[]{:S(2)}, u32[]{:S(2)}) collective-permute-start(f32[1024,128]{1,0:T(8,128)S(1)} %bitcast.17), channel_id=1, source_target_pairs={{0,2},{1,3},{32,34},{33,35},{64,66},{65,67},{96,98},{97,99},{128,1... | collective-permute-start | bytes 1572872 | tf_op jit(solution)/shard_map/ppermute | solution.py:317
  12.3 6.4 %collective-permute-start.1 = (f32[512,128]{1,0:T(8,128)S(1)}, f32[512,128]{1,0:T(8,128)S(1)}, u32[]{:S(2)}, u32[]{:S(2)}) collective-permute-start(f32[512,128]{1,0:T(8,128)S(1)} %broadcast_select_fusion.3), channel_id=1, source_target_pairs={{0,256},{32,288},{64,320},{96,352},{2,258},{34,290},{66,322},{98,3... | collective-permute-start | bytes 786440 | tf_op jit(solution)/shard_map/ppermute | solution.py:320
  22.9 5.3 %collective-permute-start.6 = (f32[1024,128]{1,0:T(8,128)S(1)}, f32[1024,128]{1,0:T(8,128)S(1)}, u32[]{:S(2)}, u32[]{:S(2)}) collective-permute-start(f32[1024,128]{1,0:T(8,128)S(1)} %collective-permute-done.5), channel_id=1, source_target_pairs={{2,10},{3,27},{34,42},{35,59},{66,74},{67,91},{98,106},{99,123},{1... | collective-permute-start | bytes 1572872 | tf_op jit(solution)/shard_map/ppermute | solution.py:317
  23.6 4.6 %collective-permute-start.2 = (f32[512,128]{1,0:T(8,128)S(1)}, f32[512,128]{1,0:T(8,128)S(1)}, u32[]{:S(2)}, u32[]{:S(2)}) collective-permute-start(f32[512,128]{1,0:T(8,128)S(1)} %broadcast_select_fusion.4), channel_id=1, source_target_pairs={{0,128},{32,160},{64,192},{96,224},{256,384},{288,416},{320,448},{... | collective-permute-start | bytes 786440 | tf_op jit(solution)/shard_map/ppermute | solution.py:320
  28.2 13.6 %copy-start.1 = (f32[512,128]{1,0:T(8,128)}, f32[512,128]{1,0:T(8,128)S(1)}, u32[]{:S(2)}) copy-start(f32[512,128]{1,0:T(8,128)S(1)} %broadcast_select_fusion.5.here) | copy-start | bytes 786436
  28.3 4.6 %collective-permute-start.7 = (f32[1024,128]{1,0:T(8,128)S(1)}, f32[1024,128]{1,0:T(8,128)S(1)}, u32[]{:S(2)}, u32[]{:S(2)}) collective-permute-start(f32[1024,128]{1,0:T(8,128)S(1)} %broadcast_select_fusion), channel_id=1, source_target_pairs={{2,26},{3,11},{10,18},{27,19},{34,58},{35,43},{42,50},{59,51},{66,... | collective-permute-start | bytes 1572872 | tf_op jit(solution)/shard_map/ppermute | solution.py:317
  29.0 5.5 %collective-permute-start.3 = (f32[128,128]{1,0:T(8,128)S(1)}, f32[128,128]{1,0:T(8,128)S(1)}, u32[]{:S(2)}, u32[]{:S(2)}) collective-permute-start(f32[128,128]{1,0:T(8,128)S(1)} %slice.14), channel_id=1, source_target_pairs={{0,32},{32,0},{64,96},{96,64},{128,160},{160,128},{192,224},{224,1... | collective-permute-start | bytes 196616 | tf_op jit(solution)/shard_map/ppermute | solution.py:320
  32.9 8.8 %collective-permute-start.8 = (f32[1024,128]{1,0:T(8,128)S(1)}, f32[1024,128]{1,0:T(8,128)S(1)}, u32[]{:S(2)}, u32[]{:S(2)}) collective-permute-start(f32[1024,128]{1,0:T(8,128)S(1)} %broadcast_select_fusion.1), channel_id=1, source_target_pairs={{2,6},{3,31},{10,14},{27,23},{18,22},{19,15},{26,30},{11,7},{34,38... | collective-permute-start | bytes 1572872 | tf_op jit(solution)/shard_map/ppermute | solution.py:317
  34.5 8.0 %copy-start.3 = (f32[2,128,128]{2,1,0:T(8,128)}, f32[2,128,128]{2,1,0:T(8,128)S(1)}, u32[]{:S(2)}) copy-start(f32[2,128,128]{2,1,0:T(8,128)S(1)} %pad_maximum_fusion.own) | copy-start | bytes 393220
  34.5 7.1 %collective-permute-start.4 = (f32[2,128,128]{2,1,0:T(8,128)S(1)}, f32[2,128,128]{2,1,0:T(8,128)S(1)}, u32[]{:S(2)}, u32[]{:S(2)}) collective-permute-start(f32[2,128,128]{2,1,0:T(8,128)S(1)} %pad_maximum_fusion.own), channel_id=1, source_target_pairs={{0,1},{1,0},{32,33},{33,32},{64,65},{65,64},{96,97},{97,96},{128,1... | collective-permute-start | bytes 393224 | tf_op jit(solution)/shard_map/ppermute | solution.py:317
  39.1 15.2 %collective-permute-start.9 = (f32[512,128]{1,0:T(8,128)S(1)}, f32[512,128]{1,0:T(8,128)S(1)}, u32[]{:S(2)}, u32[]{:S(2)}) collective-permute-start(f32[512,128]{1,0:T(8,128)S(1)} %broadcast_select_fusion.5.here), channel_id=1, source_target_pairs={{0,32},{32,0},{64,96},{96,64},{128,160},{160,128},{192,224},{224,1... | collective-permute-start | bytes 786440 | tf_op jit(solution)/shard_map/ppermute | solution.py:320
  41.7 0.8 copy-start.9
  41.8 26.0 %collective-permute-start.16 = (f32[1024,128]{1,0:T(8,128)S(1)}, f32[1024,128]{1,0:T(8,128)S(1)}, u32[]{:S(2)}, u32[]{:S(2)}) collective-permute-start(f32[1024,128]{1,0:T(8,128)S(1)} %broadcast_select_fusion.2), channel_id=1, source_target_pairs={{2,4},{6,8},{31,29},{10,12},{27,25},{14,16},{23,21},{18,20},{19,17... | collective-permute-start | bytes 1572872 | tf_op jit(solution)/shard_map/ppermute | solution.py:317
  54.4 19.8 %copy-start.5 = (f32[512,128]{1,0:T(8,128)}, f32[512,128]{1,0:T(8,128)S(1)}, u32[]{:S(2)}) copy-start(f32[512,128]{1,0:T(8,128)S(1)} %collective-permute-done.9.there) | copy-start | bytes 786436
  54.4 4.0 %collective-permute-start.12 = (f32[264,128]{1,0:T(8,128)}, f32[264,128]{1,0:T(8,128)S(1)}, u32[]{:S(2)}, u32[]{:S(2)}) collective-permute-start(f32[264,128]{1,0:T(8,128)} %get-tuple-element.51), channel_id=1, source_target_pairs={{0,24},{1,9},{32,56},{33,41},{64,88},{65,73},{96,120},{97,105},{12... | collective-permute-start | bytes 405512 | tf_op jit(solution)/shard_map/ppermute | solution.py:317
  55.7 4.2 %collective-permute-start.11 = (f32[264,128]{1,0:T(8,128)}, f32[264,128]{1,0:T(8,128)S(1)}, u32[]{:S(2)}, u32[]{:S(2)}) collective-permute-start(f32[264,128]{1,0:T(8,128)} %get-tuple-element.51), channel_id=1, source_target_pairs={{0,8},{1,25},{32,40},{33,57},{64,72},{65,89},{96,104},{97,121},{12... | collective-permute-start | bytes 405512 | tf_op jit(solution)/shard_map/ppermute | solution.py:317
  57.0 5.0 %collective-permute-start.10 = (f32[264,128]{1,0:T(8,128)}, f32[264,128]{1,0:T(8,128)S(1)}, u32[]{:S(2)}, u32[]{:S(2)}) collective-permute-start(f32[264,128]{1,0:T(8,128)} %get-tuple-element.51), channel_id=1, source_target_pairs={{0,16},{1,17},{32,48},{33,49},{64,80},{65,81},{96,112},{97,113},{1... | collective-permute-start | bytes 405512 | tf_op jit(solution)/shard_map/ppermute | solution.py:317
  62.9 11.3 %copy-start.2 = (f32[264,128]{1,0:T(8,128)}, f32[264,128]{1,0:T(8,128)S(1)}, u32[]{:S(2)}) copy-start(f32[264,128]{1,0:T(8,128)S(1)} %select_select_fusion.1.held) | copy-start | bytes 405508
  62.9 4.9 %collective-permute-start.15 = (f32[264,128]{1,0:T(8,128)S(1)}, f32[264,128]{1,0:T(8,128)S(1)}, u32[]{:S(2)}, u32[]{:S(2)}) collective-permute-start(f32[264,128]{1,0:T(8,128)S(1)} %select_select_fusion.1.held), channel_id=1, source_target_pairs={{0,6},{1,27},{8,14},{25,19},{16,22},{17,11},{24,30},{9,3},{32,38},... | collective-permute-start | bytes 405512 | tf_op jit(solution)/shard_map/ppermute | solution.py:317
  65.2 3.4 %collective-permute-start.14 = (f32[264,128]{1,0:T(8,128)S(1)}, f32[264,128]{1,0:T(8,128)S(1)}, u32[]{:S(2)}, u32[]{:S(2)}) collective-permute-start(f32[264,128]{1,0:T(8,128)S(1)} %select_select_fusion.1.held), channel_id=1, source_target_pairs={{0,2},{1,31},{8,10},{25,23},{16,18},{17,15},{24,26},{9,7},{32,34},... | collective-permute-start | bytes 405512 | tf_op jit(solution)/shard_map/ppermute | solution.py:317
  66.5 3.5 %collective-permute-start.13 = (f32[264,128]{1,0:T(8,128)S(1)}, f32[264,128]{1,0:T(8,128)S(1)}, u32[]{:S(2)}, u32[]{:S(2)}) collective-permute-start(f32[264,128]{1,0:T(8,128)S(1)} %select_select_fusion.1.held), channel_id=1, source_target_pairs={{0,4},{1,29},{8,12},{25,21},{16,20},{17,13},{24,28},{9,5},{32,36},... | collective-permute-start | bytes 405512 | tf_op jit(solution)/shard_map/ppermute | solution.py:317
  67.8 6.3 %copy-start.6 = (f32[264,128]{1,0:T(8,128)}, f32[264,128]{1,0:T(8,128)S(1)}, u32[]{:S(2)}) copy-start(f32[264,128]{1,0:T(8,128)S(1)} %collective-permute-done.15.three) | copy-start | bytes 405508
  68.6 5.6 %copy-start.7 = (f32[264,128]{1,0:T(8,128)}, f32[264,128]{1,0:T(8,128)S(1)}, u32[]{:S(2)}) copy-start(f32[264,128]{1,0:T(8,128)S(1)} %collective-permute-done.14.one) | copy-start | bytes 405508
  70.0 4.2 %copy-start.8 = (f32[264,128]{1,0:T(8,128)}, f32[264,128]{1,0:T(8,128)S(1)}, u32[]{:S(2)}) copy-start(f32[264,128]{1,0:T(8,128)S(1)} %collective-permute-done.13.two) | copy-start | bytes 405508
  70.1 4.1 %copy-start = (f32[1024,128]{1,0:T(8,128)}, f32[1024,128]{1,0:T(8,128)S(1)}, u32[]{:S(2)}) copy-start(f32[1024,128]{1,0:T(8,128)S(1)} %select_select_fusion.own) | copy-start | bytes 1572868
  70.1 4.1 %collective-permute-start.17 = (f32[1024,128]{1,0:T(8,128)S(1)}, f32[1024,128]{1,0:T(8,128)S(1)}, u32[]{:S(2)}, u32[]{:S(2)}) collective-permute-start(f32[1024,128]{1,0:T(8,128)S(1)} %select_select_fusion.own), channel_id=1, source_target_pairs={{0,1},{1,0},{2,3},{3,2},{4,5},{5,4},{6,7},{7,6},{8,9},{9,8},{10,11... | collective-permute-start | bytes 1572872 | tf_op jit(solution)/shard_map/ppermute | solution.py:317
  74.2 0.8 copy-start.4
